TPU v7x, 32 devices: a whole 2x2x4 slice. The times are simulated.
32 devices in a mesh: ctx: 8 (over y, x, core), fsdp: 4 (over z).
Axes of the slice: x: 2, y: 2, z: 4, core: 2. Of those that a mesh axis runs over, the one named last changes fastest.
Arguments:
- tokens: bfloat16 [4096, 960], P(('ctx', 'fsdp')), may hold values from -6 to 6
- pair_order: int32 [32], replicated, may hold values from 0 to 31, each once
- gain_attn: bfloat16 [960], P('fsdp'), may hold values from 0.5 to 1.5
- gain_mlp: bfloat16 [960], P('fsdp'), may hold values from 0.5 to 1.5
- w_query: bfloat16 [960, 960], P('fsdp'), may hold values from -0.3125 to 0.3125
- w_key: bfloat16 [960, 320], P('fsdp'), may hold values from -0.3125 to 0.3125
- w_value: bfloat16 [960, 320], P('fsdp'), may hold values from -0.1875 to 0.1875
- w_out: bfloat16 [960, 960], P('fsdp'), may hold values from -0.75 to 0.75
- w_gate: bfloat16 [960, 2560], P('fsdp'), may hold values from -0.1875 to 0.1875
- w_up: bfloat16 [960, 2560], P('fsdp'), may hold values from -0.1875 to 0.1875
- w_down: bfloat16 [2560, 960], P('fsdp'), may hold values from -0.125 to 0.125
- cotangent: bfloat16 [4096, 960], P(('ctx', 'fsdp')), may hold values from -6 to 6
Outputs:
- layer_out: bfloat16 [4096, 960], P(('ctx', 'fsdp'))
- grad_tokens: float32 [4096, 960], P(('ctx', 'fsdp'))
- grad_gain_attn: float32 [960], P('fsdp')
- grad_gain_mlp: float32 [960], P('fsdp')
- grad_w_query: float32 [960, 960], P('fsdp')
- grad_w_key: float32 [960, 320], P('fsdp')
- grad_w_value: float32 [960, 320], P('fsdp')
- grad_w_out: float32 [960, 960], P('fsdp')
- grad_w_gate: float32 [960, 2560], P('fsdp')
- grad_w_up: float32 [960, 2560], P('fsdp')
- grad_w_down: float32 [2560, 960], P('fsdp')
Inputs may be any that keep to these rules, and one draw needn't show every extreme that they name: Slot d holds sequence blocks pair_order[d] and 63 - pair_order[d]; each value appears once.
All inputs are finite; a program needn't handle non-finite values.
Results may differ from a plain program's by a relative error of at most 0.025.
Values may be sent and summed in bfloat16 or wider, within the bound.
No kernel may reach another device: no remote copies, remote signals or barrier semaphores. Data moves between devices by JAX's collectives and lax.ppermute only.
A program may use at most 256 MiB of HBM per device.

v0:
```python
import functools

import jax
import jax.numpy as jnp
from jax import lax
from jax.experimental import pallas as pl
from jax.experimental.pallas import tpu as pltpu
from jax.sharding import PartitionSpec as P

HEADS = 15
KV_HEADS = 5
HEAD = 64
TP = 8
GROUP = HEADS // KV_HEADS
OWN = 2 * HEAD
epsilon = 1e-05
base_theta = 100000.0
far_below = -1e30
f32 = jnp.float32
bf16 = jnp.bfloat16
i32 = jnp.int32
AXES = ("ctx", "fsdp")
MIB = 1024 * 1024
smem = pl.BlockSpec(memory_space=pltpu.SMEM)
vmem = pl.BlockSpec(memory_space=pltpu.VMEM)


def exchange(array, mask, count):
    return lax.ppermute(array, AXES, [(i, i ^ mask) for i in range(count)])


def nn(left, right):
    return lax.dot_general(left, right, (((1,), (0,)), ((), ())), preferred_element_type=f32)


def tn(left, right):
    return lax.dot_general(left, right, (((0,), (0,)), ((), ())), preferred_element_type=f32)


def nt(left, right):
    return lax.dot_general(left, right, (((1,), (1,)), ((), ())), preferred_element_type=f32)


def shape(dims, dtype):
    return jax.ShapeDtypeStruct(dims, dtype)


def call(kernel, outs, inputs, scalars=1, scratch=(), limit=56, cost=1.0, far=(), far_out=()):
    specs = [smem] * scalars + [vmem] * (len(inputs) - scalars)
    for i in far:
        specs[i] = pl.BlockSpec(memory_space=pltpu.HBM)
    out_specs = [vmem for unused in outs]
    for i in far_out:
        out_specs[i] = pl.BlockSpec(memory_space=pltpu.HBM)
    return pl.pallas_call(
        kernel,
        out_shape=tuple(outs),
        in_specs=specs,
        out_specs=tuple(out_specs),
        scratch_shapes=list(scratch),
        compiler_params=pltpu.CompilerParams(vmem_limit_bytes=limit * MIB),
        cost_estimate=pl.CostEstimate(
            flops=int(cost * 1e9), bytes_accessed=int(cost * 1e6), transcendentals=0
        ),
    )(*inputs)


def one_hot(rows, columns, start):
    row = lax.broadcasted_iota(i32, (rows, columns), 0)
    column = lax.broadcasted_iota(i32, (rows, columns), 1)
    return jnp.where(row == column + start, 1.0, 0.0).astype(bf16)


def query_positions(base_ref, at, width, half_rows):
    lane = lax.broadcasted_iota(i32, (1, width), 1)
    place = jnp.zeros((1, width), i32)
    for block in range(width // half_rows):
        start = base_ref[at + block] - block * half_rows
        place = jnp.where(lane >= block * half_rows, start + lane, place)
    return place


def key_positions(base_ref, row, at, count, half_rows, width):
    offset = lax.broadcasted_iota(i32, (half_rows, width), 0)
    return jnp.concatenate([offset + base_ref[row, at + b] for b in range(count)], axis=0)


def swap_halves(matrix):
    lane = lax.broadcasted_iota(i32, matrix.shape, 1)
    ahead = pltpu.roll(matrix, matrix.shape[1] - HEAD // 2, 1)
    behind = pltpu.roll(matrix, HEAD // 2, 1)
    return jnp.where(lane % HEAD < HEAD // 2, ahead, behind)


def norm_scale(matrix):
    return lax.rsqrt(jnp.mean(matrix * matrix, axis=1, keepdims=True) + epsilon)


def slice_attention_weights(at, w_query, w_key, w_value, w_out, gain_one, gain_two):
    d_rows, width = w_query.shape
    lanes = 2 * OWN + OWN
    rest = width - (TP - 1) * OWN

    def kernel(at_ref, q_ref, k_ref, v_ref, o_ref, g1_ref, g2_ref, out_ref, cols, heads, whole, sems):
        tp = at_ref[0]
        kv = at_ref[2]
        wides, narrows = (q_ref, o_ref), (k_ref, v_ref)

        columns = pl.ds(pl.multiple_of(tp * OWN, OWN), OWN)
        rows = pl.ds(pl.multiple_of(kv * HEAD, HEAD), HEAD)

        def wide_copies():
            return [
                pltpu.make_async_copy(ref.at[:, columns], cols.at[i], sems.at[i])
                for i, ref in enumerate(wides)
            ]

        def whole_copies():
            return [
                pltpu.make_async_copy(ref, whole.at[i], sems.at[i]) for i, ref in enumerate(wides)
            ]

        def head_copies():
            return [
                pltpu.make_async_copy(ref.at[rows, :], heads.at[i], sems.at[2 + i])
                for i, ref in enumerate(narrows)
            ]

        @pl.when(tp < TP - 1)
        def most():
            for copy in wide_copies():
                copy.start()

        @pl.when(tp == TP - 1)
        def last():
            for copy in whole_copies():
                copy.start()

        @pl.when(kv < KV_HEADS)
        def real():
            for copy in head_copies():
                copy.start()

        @pl.when(kv >= KV_HEADS)
        def none():
            heads[...] = jnp.zeros_like(heads)

        @pl.when(tp < TP - 1)
        def most_came():
            for copy in wide_copies():
                copy.wait()

        @pl.when(tp == TP - 1)
        def last_came():
            for copy in whole_copies():
                copy.wait()
            for i in range(2):
                cols[i] = jnp.zeros((d_rows, OWN), bf16)
                cols[i, :, pl.ds(0, rest)] = whole[i, :, pl.ds(width - rest, rest)]

        @pl.when(kv < KV_HEADS)
        def real_came():
            for copy in head_copies():
                copy.wait()

        out_ref[pl.ds(0, d_rows), pl.ds(0, OWN)] = cols[0]
        turned = jnp.concatenate([heads[0], heads[1]], axis=0).astype(f32).T
        out_ref[pl.ds(0, d_rows), pl.ds(OWN, OWN)] = turned.astype(bf16)
        out_ref[pl.ds(0, d_rows), pl.ds(2 * OWN, OWN)] = cols[1]
        out_ref[pl.ds(d_rows, 16), :] = jnp.zeros((16, lanes), bf16)
        out_ref[d_rows, pl.ds(0, d_rows)] = g1_ref[...]
        out_ref[d_rows + 1, pl.ds(0, d_rows)] = g2_ref[...]

    return call(
        kernel,
        [shape((d_rows + 16, lanes), bf16)],
        [at, w_query, w_key.T, w_value.T, w_out, gain_one, gain_two],
        scratch=[
            pltpu.VMEM((2, d_rows, OWN), bf16),
            pltpu.VMEM((2, HEAD, d_rows), bf16),
            pltpu.VMEM((2, d_rows, width), bf16),
            pltpu.SemaphoreType.DMA((4,)),
        ],
        limit=60,
        cost=2.0,
        far=(1, 2, 3, 4),
    )[0]


def slice_ff_weights(at, w_gate, w_up, w_down, nz):
    d_rows = w_gate.shape[0]
    ff_z, width = w_down.shape
    part = ff_z // TP
    own = part * nz


    def kernel(at_ref, g_ref, u_ref, d_ref, out_ref):
        pick = one_hot(ff_z, part, at_ref[0] * part)
        for ref, start in ((g_ref, 0), (u_ref, own)):
            pieces = [nn(ref[:, pl.ds(s * ff_z, ff_z)], pick) for s in range(nz)]
            out_ref[:, pl.ds(start, own)] = jnp.concatenate(pieces, axis=1).astype(bf16)
        pieces = [nn(d_ref[pl.ds(s * d_rows, d_rows), :], pick) for s in range(nz)]
        out_ref[:, pl.ds(2 * own, own)] = jnp.concatenate(pieces, axis=1).astype(bf16)

    return call(
        kernel,
        [shape((d_rows, 3 * own), bf16)],
        [at, w_gate, w_up, w_down.T],
        limit=16,
        cost=4.0,
    )[0]


def project_keys(at, tokens, packs, cosine, sine, cotangent):
    local, width = tokens[0].shape
    half_rows = local // 2
    rows = TP * local
    nz = len(packs)
    pack_rows, lanes = packs[0].shape
    d_rows = pack_rows - 16
    per = 4
    tiles = 2 * TP // per

    def kernel(at_ref, *refs):
        toks, refs = refs[:TP], refs[TP:]
        pack, refs = refs[:nz], refs[nz:]
        cos_ref, sin_ref, cot_ref, hid_ref, kv_ref, w_ref, side_ref, gain_ref, hold, kept, sems = refs
        z = at_ref[1]
        for s in range(nz):
            hold[z ^ s] = pack[s][...]
        for s in range(nz):
            w_ref[pl.ds(s * d_rows, d_rows), :] = hold[s, pl.ds(0, d_rows), pl.ds(0, 2 * OWN)]
        gains = [hold[s, pl.ds(d_rows, 16), pl.ds(0, d_rows)].astype(f32) for s in range(nz)]
        gain_ref[...] = jnp.concatenate(gains, axis=1)[:8]
        gain = gain_ref[pl.ds(0, 1), :]
        side_ref[pl.ds(0, local), pl.ds(0, width)] = cot_ref[...]
        turned = [
            hold[s, pl.ds(0, d_rows), pl.ds(2 * OWN, OWN)].astype(f32) for s in range(nz)
        ]
        side_ref[pl.ds(local, OWN), pl.ds(0, width)] = jnp.concatenate(turned, axis=0).T.astype(bf16)
        copies = []
        for tile in range(tiles):
            side, first = (tile * per) // TP, (tile * per) % TP
            at_rows = pl.ds(tile * per * half_rows, per * half_rows)
            block = jnp.concatenate(
                [toks[first + j][pl.ds(side * half_rows, half_rows), :] for j in range(per)], axis=0
            )
            inputs = block.astype(f32)
            hidden = (inputs * norm_scale(inputs) * gain).astype(bf16)
            kept[at_rows, :] = hidden
            copy = pltpu.make_async_copy(kept.at[at_rows, :], hid_ref.at[at_rows, :], sems.at[tile])
            copy.start()
            copies.append(copy)
            pair = nn(hidden, w_ref[:, pl.ds(OWN, OWN)])
            turned = pair * cos_ref[at_rows, :] + swap_halves(pair) * sin_ref[at_rows, :]
            lane = lax.broadcasted_iota(i32, pair.shape, 1)
            kv_ref[at_rows, :] = jnp.where(lane < HEAD, turned, pair).astype(bf16)
        for copy in copies:
            copy.wait()

    return call(
        kernel,
        [
            shape((rows, width), bf16),
            shape((rows, OWN), bf16),
            shape((width, 2 * OWN), bf16),
            shape((local + OWN, TP * OWN), bf16),
            shape((8, width), f32),
        ],
        [at, *tokens, *packs, cosine, sine, cotangent],
        scratch=[
            pltpu.VMEM((nz, pack_rows, lanes), bf16),
            pltpu.VMEM((rows, width), bf16),
            pltpu.SemaphoreType.DMA((tiles,)),
        ],
        limit=30,
        cost=4.0,
        far_out=(0,),
    )


def project_queries(tokens, hidden, w_qkv, cosine, sine):
    local, width = tokens[0].shape
    half_rows = local // 2
    rows = TP * local
    per = 4

    def kernel(*refs):
        toks, refs = refs[:TP], refs[TP:]
        hid_ref, w_ref, cos_ref, sin_ref, x_ref, qt_ref = refs
        for tile in range(2 * TP // per):
            side, first = (tile * per) // TP, (tile * per) % TP
            at_rows = pl.ds(tile * per * half_rows, per * half_rows)
            for j in range(per):
                x_ref[pl.ds((tile * per + j) * half_rows, half_rows), :] = toks[first + j][
                    pl.ds(side * half_rows, half_rows), :
                ]
            query = nn(hid_ref[at_rows, :], w_ref[:, pl.ds(0, OWN)])
            query = query * cos_ref[at_rows, :] + swap_halves(query) * sin_ref[at_rows, :]
            qt_ref[:, at_rows] = (query.astype(bf16).astype(f32) * HEAD**-0.5).T.astype(bf16)

    return call(
        kernel,
        [shape((rows, width), bf16), shape((OWN, rows), bf16)],
        [*tokens, hidden, w_qkv, cosine, sine],
        scalars=0,
        limit=30,
        cost=4.0,
    )


def attention_forward(select, key_base, query_base, turned_query, own_kv, other_kv, half_rows):
    groups = len(own_kv)
    rows = own_kv[0].shape[0]
    half = rows // 2
    blocks = half // half_rows
    wide, deep = 128, 128

    def kernel(sel_ref, key_ref, query_ref, q_ref, *refs):
        own, other = refs[:groups], refs[groups : 2 * groups]
        out_ref, low_ref, lse_ref, kv_ref, kvt_ref, top_ref, mass_ref, place_ref = refs[2 * groups :]
        for head in range(2):
            chosen = sel_ref[head] == 0
            for group in range(groups):

                @pl.when(chosen)
                def take_own():
                    kv_ref[head, group] = own[group][...]
                    kvt_ref[head, group] = own[group][...].T

                @pl.when(jnp.logical_not(chosen))
                def take_other():
                    kv_ref[head, group] = other[group][...]
                    kvt_ref[head, group] = other[group][...].T

        top_ref[...] = jnp.full_like(top_ref, far_below)
        mass_ref[...] = jnp.zeros_like(mass_ref)
        out_ref[...] = jnp.zeros_like(out_ref)

        def one_step(step, unused):
            group, head = step // 2, lax.rem(step, 2)
            row = sel_ref[head] * groups + group
            own_rows = pl.ds(pl.multiple_of(head * HEAD, HEAD), HEAD)
            place_ref[...] = key_positions(key_ref, row, 0, 2 * blocks, half_rows, 128)
            for k_start in range(0, rows, deep):
                keys_at = pl.ds(k_start, deep)
                k_side = k_start // half
                block = kv_ref[head, group, keys_at, :]
                values = kvt_ref[head, group, pl.ds(HEAD, HEAD), keys_at]
                for start in range(k_side * half, rows, wide):
                    lanes = pl.ds(start, wide)
                    turned = q_ref[own_rows, lanes]
                    padded = jnp.concatenate([turned, jnp.zeros_like(turned)], axis=0)
                    scores = nn(block, padded)
                    if start // half == k_side:
                        places = query_positions(
                            query_ref, start // half_rows, wide, half_rows
                        )
                        scores = jnp.where(place_ref[keys_at, :] <= places, scores, far_below)
                    before = top_ref[head, :, lanes]
                    top = jnp.maximum(before, jnp.max(scores, axis=0, keepdims=True))
                    weights = jnp.exp(scores - top)
                    fade = jnp.exp(before - top)
                    top_ref[head, :, lanes] = top
                    mass_ref[head, :, lanes] = mass_ref[head, :, lanes] * fade + jnp.sum(
                        weights, axis=0, keepdims=True
                    )
                    out_ref[own_rows, lanes] = out_ref[own_rows, lanes] * fade + nn(
                        values, weights.astype(bf16)
                    )
            return unused

        lax.fori_loop(0, 2 * groups, one_step, 0)
        for head in range(2):
            own_rows = pl.ds(head * HEAD, HEAD)
            mass = mass_ref[head]
            out_ref[own_rows, :] = out_ref[own_rows, :] / mass
            lse_ref[pl.ds(head, 1), :] = top_ref[head] + jnp.log(mass)
        low_ref[...] = out_ref[...].T.astype(bf16)

    return call(
        kernel,
        [shape((OWN, rows), f32), shape((rows, OWN), bf16), shape((2, rows), f32)],
        [select, key_base, query_base, turned_query, *own_kv, *other_kv],
        scalars=3,
        scratch=[
            pltpu.VMEM((2, groups, rows, OWN), bf16),
            pltpu.VMEM((2, groups, OWN, rows), bf16),
            pltpu.VMEM((2, 1, rows), f32),
            pltpu.VMEM((2, 1, rows), f32),
            pltpu.VMEM((rows, 128), i32),
        ],
        limit=36,
        cost=14.0,
    )


def attention_backward(
    select, key_base, query_base, turned_query, own_kv, other_kv, traded, attended, log_mass, half_rows
):
    groups = len(own_kv)
    rows = own_kv[0].shape[0]
    half = rows // 2
    blocks = half // half_rows
    wide, deep = 512, 256

    def kernel(sel_ref, key_ref, query_ref, q_ref, *refs):
        own, other = refs[:groups], refs[groups : 2 * groups]
        refs = refs[2 * groups :]
        local = 2 * half_rows
        parts = [refs[0], refs[1]] + [
            refs[2 + j].at[pl.ds(k * local, local), :] for j in range(TP // 2 - 1) for k in range(2)
        ]
        refs = refs[1 + TP // 2 :]
        att_ref, lse_ref, dq_ref, keep_ref, pass_ref, gb_ref = refs[:6]
        kv_ref, sum_ref, g_ref, rq_ref, rg_ref, delta_ref, pos_ref = refs[6:]
        for group in range(groups):
            kv_ref[0, group] = own[group][...]
            kv_ref[1, group] = other[group][...]
        sum_ref[...] = jnp.zeros_like(sum_ref)
        dq_ref[...] = jnp.zeros_like(dq_ref)
        zeros = jnp.zeros((rows, HEAD), bf16)
        for j in range(0, TP, 2):
            for side in range(2):
                at = pl.ds(side * half + j * half_rows, 2 * half_rows)
                pair = jnp.concatenate(
                    [parts[j + k][pl.ds(side * half_rows, half_rows), :] for k in range(2)], axis=0
                )
                g_ref[:, at] = pair[:, :OWN].T
                gb_ref[at, :] = pair[:, OWN:]
        for head in range(2):
            own_rows = pl.ds(head * HEAD, HEAD)
            rq_ref[head] = jnp.concatenate([q_ref[own_rows, :].T, zeros], axis=1)
            grad = g_ref[own_rows, :]
            rg_ref[head] = jnp.concatenate([zeros, grad.T], axis=1)
            delta_ref[pl.ds(head, 1), :] = jnp.sum(
                grad.astype(f32) * att_ref[own_rows, :], axis=0, keepdims=True
            )

        def one_group(group, unused):
            for head in range(2):
                which = sel_ref[head]
                own_rows = pl.ds(head * HEAD, HEAD)
                stat = pl.ds(head, 1)
                pos_ref[...] = key_positions(
                    key_ref, which * groups + group, 0, 2 * blocks, half_rows, 128
                )
                for k_start in range(0, rows, deep):
                    keys_at = pl.ds(k_start, deep)
                    k_side = k_start // half
                    block = kv_ref[which, group, keys_at, :]
                    turned_keys = block.T[:HEAD]
                    for start in range(k_side * half, rows, wide):
                        lanes = pl.ds(start, wide)
                        turned = q_ref[own_rows, lanes]
                        padded = jnp.concatenate([turned, jnp.zeros_like(turned)], axis=0)
                        scores = nn(block, padded)
                        if start // half == k_side:
                            places = query_positions(
                                query_ref, start // half_rows, wide, half_rows
                            )
                            at = jnp.concatenate([pos_ref[keys_at, :]] * (wide // 128), axis=1)
                            scores = jnp.where(at <= places, scores, far_below)
                        probs = jnp.exp(scores - lse_ref[stat, lanes])
                        grads = g_ref[own_rows, lanes]
                        padded = jnp.concatenate([jnp.zeros_like(grads), grads], axis=0)
                        grad_probs = nn(block, padded)
                        grad_scores = probs * (grad_probs - delta_ref[stat, lanes])
                        probs = probs.astype(bf16)
                        grad_scores = grad_scores.astype(bf16)
                        sum_ref[which, group, keys_at, :] += nn(
                            grad_scores, rq_ref[head, lanes, :]
                        ) + nn(probs, rg_ref[head, lanes, :])
                        dq_ref[own_rows, lanes] += nn(turned_keys, grad_scores)
            return unused

        lax.fori_loop(0, groups, one_group, 0)
        for group in range(groups):
            keep_ref[pl.ds(group * rows, rows), :] = sum_ref[0, group]
            pass_ref[pl.ds(group * rows, rows), :] = sum_ref[1, group].astype(bf16)

    return call(
        kernel,
        [
            shape((OWN, rows), f32),
            shape((groups * rows, OWN), f32),
            shape((groups * rows, OWN), bf16),
            shape((rows, OWN), bf16),
        ],
        [
            select,
            key_base,
            query_base,
            turned_query,
            *own_kv,
            *other_kv,
            *traded,
            attended,
            log_mass,
        ],
        scalars=3,
        scratch=[
            pltpu.VMEM((2, groups, rows, OWN), bf16),
            pltpu.VMEM((2, groups, rows, OWN), f32),
            pltpu.VMEM((OWN, rows), bf16),
            pltpu.VMEM((2, rows, OWN), bf16),
            pltpu.VMEM((2, rows, OWN), bf16),
            pltpu.VMEM((2, rows), f32),
            pltpu.VMEM((rows, 128), i32),
        ],
        limit=28,
        cost=18.0,
    )


def store_blocks(part, tile, per, half_rows, keep_ref, pass_ref, x_first=False):
    side = (tile * per) // TP
    first = lax.rem(tile * per, TP) // 2
    for j in range(per):
        piece = part[j * half_rows : (j + 1) * half_rows]
        place = first // 2 + j if x_first else first + j // 2
        if x_first and j % 2:
            place = first // 2 + j - 1
        row = (2 * place + side) * half_rows
        at = pl.ds(pl.multiple_of(row, half_rows), half_rows)
        target = keep_ref if j % 2 == 0 else pass_ref
        target[at, pl.ds(0, piece.shape[1])] = piece.astype(target.dtype)


def feed_forward(at, inputs, attended, sides, packs, gains, nz):
    rows, width = inputs.shape
    local = rows // TP
    half_rows = local // 2
    half = rows // 2
    d_rows, lanes = packs[0].shape
    ff = lanes // 3
    part_rows = ff // nz
    per = 4
    tile_rows = per * half_rows
    tiles = 2 * TP // per

    def kernel(at_ref, x_ref, *refs):
        att, refs = refs[:TP], refs[TP:]
        extra, refs = refs[:TP], refs[TP:]
        pack, refs = refs[:nz], refs[nz:]
        gain_ref, refs = refs[0], refs[1:]
        resid_out, gk_ref, gp_ref, gain_out, dn_w = refs[:5]
        targets, prod_out, refs = refs[5 : 5 + nz], refs[5 + nz], refs[6 + nz :]
        att_ref, wo_ref, gu_w, cot_ref, hold, acc_gu, acc_dn, blocks, prod_ref, sems = refs
        tp = at_ref[0]
        z = at_ref[1]
        for j in range(TP):
            columns = pl.ds(pl.multiple_of((tp ^ j) * OWN, OWN), OWN)
            wo_ref[columns, :] = extra[j][pl.ds(local, OWN), pl.ds(0, width)]
            for side in range(2):
                for k in range(TP):
                    att_ref[pl.ds(side * half + k * half_rows, half_rows), columns] = att[j][
                        pl.ds(side * half + (k ^ j) * half_rows, half_rows), :
                    ]
                cot_ref[pl.ds(side * half + j * half_rows, half_rows), :] = extra[j][
                    pl.ds(side * half_rows, half_rows), pl.ds(0, width)
                ]
        for s in range(nz):
            hold[z ^ s] = pack[s][...]
        for s in range(nz):
            rows_at = pl.ds(s * d_rows, d_rows)
            gu_w[rows_at, :] = hold[s, :, pl.ds(0, 2 * ff)]
            dn_w[rows_at, :] = jnp.concatenate(
                [
                    hold[b][:, 2 * ff + s * part_rows : 2 * ff + (s + 1) * part_rows]
                    for b in range(nz)
                ],
                axis=1,
            )
        gain = gain_ref[pl.ds(1, 1), :]
        gain_out[...] = jnp.zeros_like(gain_out)
        acc_gu[...] = jnp.zeros_like(acc_gu)
        acc_dn[...] = jnp.zeros_like(acc_dn)

        def copy_of(tile):
            at_rows = pl.ds(pl.multiple_of(tile * tile_rows, tile_rows), tile_rows)
            return pltpu.make_async_copy(
                prod_ref.at[at_rows, :], prod_out.at[at_rows, :], sems.at[tile]
            )

        def one_tile(tile, unused):
            at_rows = pl.ds(pl.multiple_of(tile * tile_rows, tile_rows), tile_rows)
            branch = nt(att_ref[at_rows, :][:, :width], wo_ref[pl.ds(0, width), :])
            resid = x_ref[at_rows, :].astype(f32) + branch
            side = (tile * per) // TP

            @pl.when(lax.rem(tile * per, TP) == 0)
            def keep_own():
                resid_out[pl.ds(pl.multiple_of(side * half_rows, half_rows), half_rows), :] = resid[
                    :half_rows
                ]

            normal = resid * norm_scale(resid)
            hidden = (normal * gain).astype(bf16)
            gate_up = nn(hidden, gu_w[...])
            gate, up = gate_up[:, :ff], gate_up[:, ff:]
            sigmoid = 1.0 / (1.0 + jnp.exp(-gate))
            activated = gate * sigmoid
            product = (activated * up).astype(bf16)
            prod_ref[at_rows, :] = product
            copy_of(tile).start()
            cotangent = cot_ref[at_rows, :]
            grad_product = nn(cotangent, dn_w[...])
            grad_gate = grad_product * up * sigmoid * (1.0 + gate * (1.0 - sigmoid))
            grad_gu = jnp.concatenate([grad_gate, grad_product * activated], axis=1).astype(bf16)
            partial = nt(grad_gu, gu_w[...])
            gain_out[pl.ds(0, 1), :] += jnp.sum(partial * normal, axis=0, keepdims=True)
            store_blocks(partial, tile, per, half_rows, gk_ref, gp_ref)
            acc_gu[...] += tn(hidden, grad_gu)
            acc_dn[...] += tn(cotangent, product)
            return unused

        lax.fori_loop(0, tiles, one_tile, 0)
        for b in range(nz):
            blocks[b] = jnp.concatenate(
                [
                    acc_dn[pl.ds(s * d_rows, d_rows), :][:, b * part_rows : (b + 1) * part_rows]
                    for s in range(nz)
                ],
                axis=1,
            )
        for s in range(nz):
            block = pl.ds(pl.multiple_of((z ^ s) * d_rows, 8), d_rows)
            targets[s][:, pl.ds(0, 2 * ff)] = acc_gu[block, :].astype(targets[s].dtype)
            targets[s][:, pl.ds(2 * ff, ff)] = blocks[z ^ s].astype(targets[s].dtype)
        for tile in range(tiles):
            copy_of(tile).wait()

    return call(
        kernel,
        [
            shape((local, width), f32),
            shape((TP // 2 * local, width), bf16),
            shape((TP // 2 * local, TP * OWN), bf16),
            shape((8, width), f32),
            shape((width, ff), bf16),
        ]
        + [shape((d_rows, lanes), f32 if s % 2 == 0 else bf16) for s in range(nz)]
        + [shape((rows, ff), bf16)],
        [at, inputs, *attended, *sides, *packs, gains],
        scratch=[
            pltpu.VMEM((rows, TP * OWN), bf16),
            pltpu.VMEM((TP * OWN, width), bf16),
            pltpu.VMEM((width, 2 * ff), bf16),
            pltpu.VMEM((rows, width), bf16),
            pltpu.VMEM((nz, d_rows, lanes), bf16),
            pltpu.VMEM((width, 2 * ff), f32),
            pltpu.VMEM((width, ff), f32),
            pltpu.VMEM((nz, d_rows, ff), f32),
            pltpu.VMEM((rows, ff), bf16),
            pltpu.SemaphoreType.DMA((tiles,)),
        ],
        limit=36,
        cost=17.0,
        far_out=(5 + nz,),
    )


def feed_forward_rest(at, attended, sides, product, w_down):
    rows = attended[0].shape[0]
    width, ff = w_down.shape
    local = rows // TP
    half_rows = local // 2
    half = rows // 2
    per = 4
    tile_rows = per * half_rows

    def kernel(at_ref, *refs):
        att, refs = refs[:TP], refs[TP:]
        extra, refs = refs[:TP], refs[TP:]
        prod_ref, dn_w, att_out, wo_out, lk_ref, lp_ref = refs
        tp = at_ref[0]
        for j in range(TP):
            columns = pl.ds(pl.multiple_of((tp ^ j) * OWN, OWN), OWN)
            wo_out[columns, :] = extra[j][pl.ds(local, OWN), pl.ds(0, width)]
            for side in range(2):
                for k in range(TP):
                    att_out[pl.ds(side * half + k * half_rows, half_rows), columns] = att[j][
                        pl.ds(side * half + (k ^ j) * half_rows, half_rows), :
                    ]

        def one_tile(tile, unused):
            at_rows = pl.ds(pl.multiple_of(tile * tile_rows, tile_rows), tile_rows)
            part = nt(prod_ref[at_rows, :], dn_w[...])
            store_blocks(part, tile, per, half_rows, lk_ref, lp_ref)
            return unused

        lax.fori_loop(0, 2 * TP // per, one_tile, 0)

    return call(
        kernel,
        [
            shape((rows, TP * OWN), bf16),
            shape((TP * OWN, width), bf16),
            shape((TP // 2 * local, width), bf16),
            shape((TP // 2 * local, TP * OWN), bf16),
        ],
        [at, *attended, *sides, product, w_down],
        limit=24,
        cost=5.0,
    )


def add_crossed(keep, crossed, count, tail=None):
    local, width = keep.shape[0] // count, keep.shape[1]
    tails = [] if tail is None else [tail]
    more = 0 if tail is None else tail.shape[0]

    def kernel(keep_ref, cross_ref, *refs):
        own_ref, *sends = refs[len(tails) :]
        for j in range(count):
            at = pl.ds(j * local, local)
            target = own_ref if j == 0 else sends[j - 1]
            target[pl.ds(0, local), pl.ds(0, width)] = (
                keep_ref[at, :].astype(f32) + cross_ref[at, pl.ds(0, width)].astype(f32)
            ).astype(target.dtype)
        if tails:
            sends[-1][pl.ds(local, more), pl.ds(0, width)] = refs[0][...]

    return call(
        kernel,
        [shape((local, width), f32)]
        + [shape((local, width), bf16)] * (count - 2)
        + [shape((local + more, TP * OWN if tails else width), bf16)],
        [keep, crossed, *tails],
        scalars=0,
        limit=12,
        cost=1.0,
    )


def branch_gradient(at, sums, resid, cotangent, w_out, gains):
    local, width = resid.shape

    def kernel(at_ref, *refs):
        parts, refs = refs[: len(sums)], refs[len(sums) :]
        resid_ref, cot_ref, wo_ref, gain_ref, grad_ref, keep_ref, pass_ref, ga_ref, gb_ref = refs
        tp = at_ref[0]
        grad_hidden = parts[0][...]
        for part in parts[1:]:
            grad_hidden = grad_hidden + part[...].astype(f32)
        resid = resid_ref[...]
        scale = norm_scale(resid)
        normal = resid * scale
        grad = grad_hidden * gain_ref[pl.ds(1, 1), :]
        grad = scale * (grad - normal * jnp.mean(grad * normal, axis=1, keepdims=True))
        grad = grad + cot_ref[...].astype(f32)
        grad_ref[...] = grad
        low = grad.astype(bf16)
        gb_ref[...] = jnp.zeros_like(gb_ref)
        gb_ref[:, pl.ds(0, width)] = low
        ga_ref[...] = jnp.zeros_like(ga_ref)
        ga_ref[:, pl.ds(0, width)] = nn(low, wo_ref[pl.ds(0, width), :]).astype(bf16)
        for j in range(TP):
            columns = pl.ds(pl.multiple_of((tp ^ j) * OWN, OWN), OWN)
            target = keep_ref if j % 2 == 0 else pass_ref
            rows = pl.ds((j // 2) * local, local)
            target[rows, pl.ds(0, OWN)] = ga_ref[:, columns]
            target[rows, pl.ds(OWN, OWN)] = gb_ref[:, columns]

    blocks = shape((TP // 2 * local, 2 * OWN), bf16)
    return call(
        kernel,
        [shape((local, width), f32), blocks, blocks],
        [at, *sums, resid, cotangent, w_out, gains],
        scratch=[pltpu.VMEM((local, TP * OWN), bf16), pltpu.VMEM((local, TP * OWN), bf16)],
        limit=16,
        cost=3.0,
    )


def pair_up(keep, crossed, count):
    local, width = keep.shape[0] // count, keep.shape[1]

    def kernel(keep_ref, cross_ref, *outs):
        for j in range(1, count):
            at = pl.ds(j * local, local)
            outs[j - 1][pl.ds(0, local), :] = keep_ref[at, :]
            outs[j - 1][pl.ds(local, local), :] = cross_ref[at, :]

    return call(
        kernel,
        [shape((2 * local, width), bf16)] * (count - 1),
        [keep, crossed],
        scalars=0,
        limit=8,
        cost=0.7,
    )


def projection_gradient(
    at, grad_query, grad_kv, inputs, hidden, w_qkv, gain_sums, cosine, sine, grad_out, nz
):
    rows, width = inputs.shape
    local = rows // TP
    half_rows = local // 2
    d_rows = width // nz
    per = 4
    tile_rows = per * half_rows
    pieces = len(grad_kv)

    def kernel(at_ref, dq_ref, *refs):
        kvs, refs = refs[:pieces], refs[pieces:]
        x_ref, hid_ref, w_ref, gain_two_ref, cos_ref, sin_ref, wo_ref = refs[:7]
        keep_ref, pass_ref, own_ref = refs[7:10]
        sends, refs = refs[10 : 10 + nz - 1], refs[10 + nz - 1 :]
        turn_ref, acc_ref, gain_acc, hold = refs
        z = at_ref[1]
        turn_ref[...] = dq_ref[...].T * HEAD**-0.5
        acc_ref[...] = jnp.zeros_like(acc_ref)
        gain_acc[...] = jnp.zeros_like(gain_acc)

        def one_tile(tile, unused):
            at_rows = pl.ds(pl.multiple_of(tile * tile_rows, tile_rows), tile_rows)
            cos, sin = cos_ref[at_rows, :], sin_ref[at_rows, :]
            query = turn_ref[at_rows, :]
            query = query * cos - swap_halves(query) * sin
            pair = kvs[0][at_rows, :].astype(f32)
            for piece in kvs[1:]:
                pair = pair + piece[at_rows, :].astype(f32)
            turned = pair * cos - swap_halves(pair) * sin
            lane = lax.broadcasted_iota(i32, pair.shape, 1)
            pair = jnp.where(lane < HEAD, turned, pair)
            grad = jnp.concatenate([query, pair], axis=1).astype(bf16)
            partial = nt(grad, w_ref[...])
            x = x_ref[at_rows, :].astype(f32)
            gain_acc[pl.ds(0, 1), :] += jnp.sum(partial * (x * norm_scale(x)), axis=0, keepdims=True)
            store_blocks(partial, tile, per, half_rows, keep_ref, pass_ref, True)
            acc_ref[...] += tn(hid_ref[at_rows, :], grad)
            return unused

        lax.fori_loop(0, 2 * TP // per, one_tile, 0)
        hold[...] = jnp.zeros_like(hold)
        for s in range(nz):
            columns = slice(s * d_rows, (s + 1) * d_rows)
            hold[s, pl.ds(0, 1), pl.ds(0, d_rows)] = gain_acc[pl.ds(0, 1), :][:, columns]
            hold[s, pl.ds(1, 1), pl.ds(0, d_rows)] = gain_two_ref[pl.ds(0, 1), :][:, columns]
        for s in range(nz):
            block = z ^ s
            target = own_ref if s == 0 else sends[s - 1]
            rows_at = pl.ds(pl.multiple_of(block * d_rows, 8), d_rows)
            part = pl.ds(0, d_rows)
            target[part, pl.ds(0, 2 * OWN)] = acc_ref[rows_at, :].astype(target.dtype)
            target[part, pl.ds(2 * OWN, OWN)] = wo_ref[rows_at, :].astype(target.dtype)
            target[pl.ds(d_rows, 16), :] = hold[block].astype(target.dtype)

    return call(
        kernel,
        [
            shape((TP // 2 * local, width), bf16),
            shape((TP // 2 * local, TP * OWN), bf16),
            shape((d_rows + 16, 3 * OWN), f32),
        ]
        + [shape((d_rows + 16, 3 * OWN), bf16)] * (nz - 1),
        [at, grad_query, *grad_kv, inputs, hidden, w_qkv, gain_sums, cosine, sine, grad_out],
        scratch=[
            pltpu.VMEM((rows, OWN), f32),
            pltpu.VMEM((width, 2 * OWN), f32),
            pltpu.VMEM((8, width), f32),
            pltpu.VMEM((nz, 16, 3 * OWN), f32),
        ],
        limit=32,
        cost=8.0,
    )


def token_gradient(sums, tokens, grad_resid, gains):
    local, width = tokens.shape

    def kernel(*refs):
        parts, refs = refs[: len(sums)], refs[len(sums) :]
        x_ref, grad_ref, gain_ref, out_ref = refs
        grad_hidden = parts[0][...]
        for part in parts[1:]:
            grad_hidden = grad_hidden + part[...].astype(f32)
        x = x_ref[...].astype(f32)
        scale = norm_scale(x)
        normal = x * scale
        grad = grad_hidden * gain_ref[pl.ds(0, 1), :]
        grad = scale * (grad - normal * jnp.mean(grad * normal, axis=1, keepdims=True))
        out_ref[...] = (grad + grad_ref[...]).T

    return call(
        kernel,
        [shape((width, local), f32)],
        [*sums, tokens, grad_resid, gains],
        scalars=0,
        limit=8,
        cost=1.0,
    )[0].T


def layer_output(near, arrived, resid):
    local, width = resid.shape
    start = arrived.shape[0] - local

    def kernel(near_ref, in_ref, resid_ref, out_ref):
        total = resid_ref[...] + near_ref[...] + in_ref[pl.ds(start, local), pl.ds(0, width)].astype(f32)
        out_ref[...] = total.T.astype(bf16)

    turned = shape(resid.shape[::-1], bf16)
    return call(kernel, [turned], [near, arrived, resid], scalars=0, limit=8, cost=1.0)[0].T


def first_sum(own, arrived):
    def kernel(own_ref, in_ref, out_ref):
        out_ref[...] = (own_ref[...] + in_ref[...].astype(f32)).astype(bf16)

    return call(
        kernel, [shape(own.shape, bf16)], [own, arrived], scalars=0, limit=8, cost=1.0
    )[0]


def last_sum(own, *arrived):
    rows, lanes = own.shape

    def kernel(own_ref, *refs):
        total = own_ref[...]
        for ref in refs[:-1]:
            total = total + ref[...].astype(f32)
        refs[-1][:, pl.ds(0, lanes)] = total.astype(bf16)

    return call(
        kernel, [shape((rows, TP * OWN), bf16)], [own, *arrived], scalars=0, limit=8, cost=1.0
    )[0]


def ff_outputs(at, mine, by_x, by_y, by_xy, odd, ff_z, nz):
    d_rows = mine.shape[0]
    part = ff_z // TP
    ff = part * nz

    def kernel(at_ref, m_ref, x_ref, y_ref, xy_ref, odd_ref, gate_ref, up_ref, down_ref, hold):
        tp = at_ref[0]
        lanes = pl.ds(0, 3 * ff)
        for j, ref in enumerate((m_ref, x_ref, y_ref, xy_ref)):
            hold[tp ^ (2 * j)] = ref[:, lanes]
        for j in range(TP // 2):
            hold[tp ^ (2 * j + 1)] = odd_ref[pl.ds(d_rows * j, d_rows), lanes]
        for s in range(nz):
            for start in (s * part, ff + s * part, 2 * ff + s * part):
                block = jnp.concatenate(
                    [hold[c][:, start : start + part] for c in range(TP)], axis=1
                ).astype(f32)
                if start < ff:
                    gate_ref[:, pl.ds(s * ff_z, ff_z)] = block
                elif start < 2 * ff:
                    up_ref[:, pl.ds(s * ff_z, ff_z)] = block
                else:
                    down_ref[pl.ds(s * d_rows, d_rows), :] = block

    gate, up, down = call(
        kernel,
        [
            shape((d_rows, nz * ff_z), f32),
            shape((d_rows, nz * ff_z), f32),
            shape((nz * d_rows, ff_z), f32),
        ],
        [at, mine, by_x, by_y, by_xy, odd],
        scratch=[pltpu.VMEM((TP, d_rows, 3 * ff), bf16)],
        limit=32,
        cost=7.0,
    )
    return gate, up, down.T


def projection_outputs(at, slots, width):
    d_rows = slots[0].shape[0] - 16

    def kernel(at_ref, *refs):
        parts, (q_ref, k_ref, v_ref, o_ref, one_ref, two_ref, hold) = refs[:TP], refs[TP:]
        tp = at_ref[0]
        total = jnp.zeros((16, 3 * OWN), f32)
        for j in range(TP):
            hold[tp ^ j] = parts[j][...].astype(f32)
            total = total + parts[j][pl.ds(d_rows, 16), :].astype(f32)
        one_ref[...] = total[0:1, :d_rows]
        two_ref[...] = total[1:2, :d_rows]
        heads = [hold[c][:d_rows, :OWN] for c in range(TP)]
        q_ref[...] = jnp.concatenate(heads, axis=1)[:, :width]
        heads = [hold[c][:d_rows, 2 * OWN :] for c in range(TP)]
        o_ref[...] = jnp.concatenate(heads, axis=1)[:, :width]
        kv = [hold[c][:d_rows, OWN : 2 * OWN] for c in range(TP)]
        kv = [kv[0], kv[1] + kv[2], kv[3] + kv[4], kv[5], kv[6]]
        for c in range(KV_HEADS):
            turned = kv[c].T
            k_ref[pl.ds(c * HEAD, HEAD), :] = turned[:HEAD]
            v_ref[pl.ds(c * HEAD, HEAD), :] = turned[HEAD:]

    query, key, value, out, one, two = call(
        kernel,
        [
            shape((d_rows, width), f32),
            shape((KV_HEADS * HEAD, d_rows), f32),
            shape((KV_HEADS * HEAD, d_rows), f32),
            shape((d_rows, width), f32),
            shape((1, d_rows), f32),
            shape((1, d_rows), f32),
        ],
        [at, *slots],
        scratch=[pltpu.VMEM((TP, d_rows + 16, 3 * OWN), f32)],
        limit=12,
        cost=0.01,
    )
    return query, key.T, value.T, out, one, two


def body(
    tokens,
    pair_order,
    gain_attn,
    gain_mlp,
    w_query,
    w_key,
    w_value,
    w_out,
    w_gate,
    w_up,
    w_down,
    cotangent,
):
    local_rows, width = tokens.shape
    half_rows = local_rows // 2
    nz = lax.axis_size("fsdp")
    outer = lax.axis_size("ctx") // TP
    count = lax.axis_size(AXES)
    groups = outer * nz
    me = lax.axis_index(AXES)
    z = lax.axis_index("fsdp")
    tp = lax.axis_index("ctx") % TP
    kv_index = (4 * (tp // 2)) // GROUP + tp % 2
    at = jnp.stack([tp, z, kv_index]).astype(i32)
    send = functools.partial(exchange, count=count)
    group_mask = [(g // nz) * TP * nz + g % nz for g in range(groups)]

    def after(value, *others):
        return lax.optimization_barrier((value, *others))[0]

    def level(*arrays):
        return list(lax.optimization_barrier(arrays))

    def gather_even(block):
        return [block] + [send(block, j * nz) for j in range(2, TP, 2)]

    def gather_odd(even):
        return [piece for e in even for piece in (e, send(e, nz))]

    def scatter_far(pieces):
        return [send(piece, 2 * (j + 1) * nz) for j, piece in enumerate(pieces)]

    def from_z(block):
        return [block] + [send(block, s) for s in range(1, nz)]

    pack_one = slice_attention_weights(at, w_query, w_key, w_value, w_out, gain_attn, gain_mlp)
    token_slots = gather_odd(level(*gather_even(tokens)))
    pack_two = slice_ff_weights(after(at, pack_one), w_gate, w_up, w_down, nz)
    pack_one = from_z(pack_one)

    slot_of = jnp.array([[m | (j * nz) for j in range(TP)] for m in group_mask], dtype=i32)
    low = pair_order[me ^ slot_of]
    base = jnp.stack([low, 2 * count - 1 - low], axis=1) * half_rows
    query_base = base[0].reshape(2 * TP)
    partner = jnp.array([j ^ 1 for j in range(TP)], dtype=i32)
    key_base = jnp.stack([base, base[:, :, partner]]).reshape(2 * groups, 2 * TP)
    places = (query_base[:, None] + jnp.arange(half_rows, dtype=i32)[None, :]).reshape(-1)
    lane = jnp.arange(OWN)
    freqs = base_theta ** (-2.0 * (lane % (HEAD // 2)).astype(f32) / HEAD)
    angles = places.astype(f32)[:, None] * freqs[None, :]
    cosine = jnp.cos(angles)
    sine = jnp.sin(angles) * jnp.where(lane % HEAD < HEAD // 2, -1.0, 1.0)[None, :]
    select = jnp.where((2 * tp + jnp.arange(2)) // GROUP == kv_index, 0, 1).astype(i32)

    mask_x, mask_y = 2 * nz, 4 * nz
    hidden_one, kv, w_qkv, side, gains = project_keys(
        after(at, pack_two, select, key_base, query_base),
        token_slots,
        pack_one,
        cosine,
        sine,
        cotangent,
    )
    own_kv = [kv] + [send(kv, m) for m in group_mask[1:]]
    side_x, side_y = send(side, mask_x), send(side, mask_y)
    inputs, turned_query = project_queries(
        token_slots, after(hidden_one, kv), w_qkv, cosine, sine
    )
    side_x, side_y, inputs, turned_query, *own_kv = level(
        side_x, side_y, inputs, turned_query, *own_kv
    )
    other_kv = level(*[send(slot, nz) for slot in own_kv])
    one, near = send(after(pack_two, *own_kv), 1), send(after(pack_two, *own_kv), 2)
    side_xy = send(side_x, mask_y)
    side_odd, odd_x = send(after(side, *other_kv), nz), send(after(side_x, *other_kv), nz)
    attended, attended_own, log_mass = attention_forward(
        select, key_base, query_base, turned_query, own_kv, other_kv, half_rows
    )
    attended_own, near, one, side_xy, side_odd, odd_x = level(
        attended_own, near, one, side_xy, side_odd, odd_x
    )
    far, side_xy, *even = level(send(near, 1), side_xy, *gather_even(attended_own))
    attended_slots = gather_odd(even)
    packs = [pack_two, one, near, far]
    odd_y = send(after(side_y, side_xy), nz)
    sides = [side, side_odd, side_x, odd_x, side_y, odd_y, side_xy, send(side_xy, nz)]

    resid, grad_keep, grad_pass, gain_sums, w_down_own, *ff_blocks, product = feed_forward(
        at, inputs, attended_slots, sides, packs, gains, nz
    )
    ff_own, ff_one, ff_two, ff_three = ff_blocks
    first, *rest = add_crossed(grad_keep, send(grad_pass, nz), TP // 2)
    attended_low, w_out_all, out_keep, out_pass, ff_three, first, *rest = level(
        *feed_forward_rest(after(at, first), attended_slots, sides, product, w_down_own),
        send(after(ff_three, first), 1),
        first,
        *scatter_far(rest),
    )
    grad_resid, trade_keep, trade_pass = branch_gradient(
        at, [first, *rest], resid, cotangent, w_out_all, gains
    )
    crossed, out_crossed = level(send(trade_pass, nz), send(after(out_pass, first), nz))
    pairs = level(*scatter_far(pair_up(trade_keep, crossed, TP // 2)))
    out_near, out_far = add_crossed(out_keep, out_crossed, 2)
    ff_one = send(after(ff_one, crossed), 1)
    ff_two = send(first_sum(ff_two, ff_three), 2)
    out_far = send(after(out_far, *pairs), mask_y)

    grad_query, kv_keep, kv_pass, branch_columns = attention_backward(
        after(select, out_near),
        key_base,
        query_base,
        turned_query,
        own_kv,
        other_kv,
        [trade_keep, crossed, *pairs],
        attended,
        log_mass,
        half_rows,
    )
    kv_pass, ff_one, ff_two, out_far = level(kv_pass, ff_one, ff_two, out_far)
    kv_crossed = send(kv_pass, nz)
    first, *rest = add_crossed(kv_keep, kv_crossed, groups)
    grad_out = tn(attended_low[:, :width], after(branch_columns, rest[0]))
    ff_total = last_sum(after(ff_own, grad_out), ff_one, ff_two)

    for step in range(outer.bit_length() - 1):
        crossing = send(ff_total, TP * nz << step).astype(f32)
        ff_total = (ff_total.astype(f32) + crossing).astype(bf16)
    out_near, out_far = add_crossed(after(out_near, rest[0]), out_far, 2)
    ff_x, ff_y, *grad_kv = level(
        send(ff_total, mask_x),
        send(ff_total, mask_y),
        *[send(piece, m) for piece, m in zip(rest, group_mask[1:])],
    )

    last_keep, last_pass, last_own, *last_sends = projection_gradient(
        at,
        grad_query,
        [first, *grad_kv],
        inputs,
        hidden_one,
        w_qkv,
        gain_sums,
        cosine,
        sine,
        grad_out,
        nz,
    )
    near, far = add_crossed(last_keep, send(last_pass, nz), 2, out_far)
    ff_xy, far, *arrived = level(
        send(after(ff_x, last_own), mask_y),
        send(far, mask_x),
        *[send(piece, s + 1) for s, piece in enumerate(last_sends)],
    )
    layer_out = layer_output(out_near, far, resid)
    near, far = add_crossed(near, far, 2)
    last_total = last_own
    for piece in arrived:
        last_total = last_total + piece.astype(f32)
    for step in range(outer.bit_length() - 1):
        last_total = last_total + send(last_total.astype(bf16), TP * nz << step).astype(f32)
    last_total = last_total.astype(bf16)
    ff_slots = [ff_total, ff_x, ff_y, ff_xy]
    ff_slots.append(send(jnp.concatenate(ff_slots, axis=0), nz))
    grad_gate, grad_up, grad_down = ff_outputs(at, *ff_slots, w_down.shape[0], nz)
    far = send(far, mask_y)
    grad_gate, *even = level(grad_gate, *gather_even(last_total))
    last_slots = gather_odd(even)
    grad_w_query, grad_w_key, grad_w_value, grad_out, gain_one, gain_two = projection_outputs(
        at, last_slots, width
    )
    grad_tokens = token_gradient([after(near, grad_w_query), far], tokens, grad_resid, gains)
    return (
        layer_out,
        grad_tokens,
        gain_one.reshape(-1),
        gain_two.reshape(-1),
        grad_w_query,
        grad_w_key,
        grad_w_value,
        grad_out,
        grad_gate,
        grad_up,
        grad_down,
    )


def solution(mesh):
    return jax.shard_map(
        body,
        mesh=mesh,
        in_specs=(
            P(("ctx", "fsdp"), None),
            P(),
            P("fsdp"),
            P("fsdp"),
            P("fsdp", None),
            P("fsdp", None),
            P("fsdp", None),
            P("fsdp", None),
            P("fsdp", None),
            P("fsdp", None),
            P("fsdp", None),
            P(("ctx", "fsdp"), None),
        ),
        out_specs=(
            P(("ctx", "fsdp"), None),
            P(("ctx", "fsdp"), None),
            P("fsdp"),
            P("fsdp"),
            P("fsdp", None),
            P("fsdp", None),
            P("fsdp", None),
            P("fsdp", None),
            P("fsdp", None),
            P("fsdp", None),
            P("fsdp", None),
        ),
        check_vma=False,
    )
```

profile of v0, /device:TPU:0, one launch (start us, length us, event | category | flops | bytes accessed | tf_op | source)
XLA Modules:
  0.0 249.1 jit_solution(6729445958772686585)
XLA Ops:
  1.3 2.5 shard_map.221.refs_8_
  3.9 5.1 %collective-permute-start.9 = (bf16[256,384]{1,0:T(8,128)(2,1)}, bf16[256,384]{1,0:T(8,128)(2,1)}, u32[]{:S(2)}, u32[]{:S(2)}) collective-permute-start(bf16[256,384]{1,0:T(8,128)(2,1)} %shard_map.221.refs_8_), channel_id=1, source_target_pairs={{0,3},{1,2},{2,1},{3,0},{4,7},{5,6},{6,5},{7,4},{8,11},{9,10},{10,... | collective-permute-start | bytes 589832 | tf_op jit(solution)/shard_map/ppermute | solution.py:29
  9.1 2.5 %collective-permute-start.2 = (bf16[128,960]{1,0:T(8,128)(2,1)S(1)}, bf16[128,960]{1,0:T(8,128)(2,1)S(1)}, u32[]{:S(2)}, u32[]{:S(2)}) collective-permute-start(bf16[128,960]{1,0:T(8,128)(2,1)S(1)} %copy.57.refs_2_), channel_id=1, source_target_pairs={{0,24},{1,25},{2,26},{3,27},{4,28},{5,29},{6,30},{7,31},{8,16},{9,... | collective-permute-start | bytes 737288 | tf_op jit(solution)/shard_map/ppermute | solution.py:29
  14.7 1.3 copy-done.5
  15.9 1.9 shard_map.222.refs_16_
  18.8 1.1 copy.62.refs_14_.refs_5_
  20.7 3.1 %collective-permute-done.1.refs_4_ = bf16[128,960]{1,0:T(8,128)(2,1)} collective-permute-done((bf16[128,960]{1,0:T(8,128)(2,1)S(1)}, bf16[128,960]{1,0:T(8,128)(2,1)}, u32[]{:S(2)}, u32[]{:S(2)}) %collective-permute-start.1) | collective-permute-done | bytes 245792 | tf_op jit(solution)/shard_map/ppermute | solution.py:29
  23.7 1.1 copy.61.refs_0_
  26.1 1.9 fusion.2
  28.0 1.6 collective-permute-done.7.refs_9_
  29.6 3.5 %shard_map.223 = (bf16[1024,960]{1,0:T(8,128)(2,1)S(1)}, bf16[1024,128]{1,0:T(8,128)(2,1)S(1)}, bf16[960,256]{1,0:T(8,128)(2,1)S(1)}, bf16[256,1024]{1,0:T(8,128)(2,1)S(1)}, f32[8,960]{1,0:T(8,128)S(1)}) custom-call(s32[3]{0:T(128)S(1)} %copy-done.2, bf16[128,960]{1,0:T(8,128)(2,1)S(1)} %copy.61.refs_0_, ...), custom_call_target="tpu_custom_call" | custom-call | flops 4000000000 | bytes 4000000 | tf_op jit(solution)/shard_map/pallas_call | solution.py:55
  33.1 1.5 collective-permute-start.11
  34.6 1.9 collective-permute-start.10
  36.5 2.4 collective-permute-start.14
  38.9 2.0 collective-permute-start.12
  40.9 2.1 shard_map.224
  43.0 4.6 %collective-permute-done.14.refs_3_ = bf16[1024,128]{1,0:T(8,128)(2,1)S(1)} collective-permute-done((bf16[1024,128]{1,0:T(8,128)(2,1)S(1)}, bf16[1024,128]{1,0:T(8,128)(2,1)S(1)}, u32[]{:S(2)}, u32[]{:S(2)}) %collective-permute-start.14) | collective-permute-done | bytes 262176 | tf_op jit(solution)/shard_map/ppermute | solution.py:29
  47.7 11.7 %collective-permute-done.13.refs_2_ = bf16[1024,128]{1,0:T(8,128)(2,1)S(1)} collective-permute-done((bf16[1024,128]{1,0:T(8,128)(2,1)S(1)}, bf16[1024,128]{1,0:T(8,128)(2,1)S(1)}, u32[]{:S(2)}, u32[]{:S(2)}) %collective-permute-start.13) | collective-permute-done | bytes 262176 | tf_op jit(solution)/shard_map/ppermute | solution.py:29
  61.0 2.6 %collective-permute-start.19 = (bf16[240,960]{1,0:T(8,128)(2,1)S(1)}, bf16[240,960]{1,0:T(8,128)(2,1)S(1)}, u32[]{:S(2)}, u32[]{:S(2)}) collective-permute-start(bf16[240,960]{1,0:T(8,128)(2,1)S(1)} %copy-done.7), channel_id=1, source_target_pairs={{0,2},{1,3},{2,0},{3,1},{4,6},{5,7},{6,4},{7,5},{8,10},{9,11},{10,... | collective-permute-start | bytes 1382408 | tf_op jit(solution)/shard_map/ppermute | solution.py:29
  63.6 1.4 collective-permute-start.21
  65.6 13.5 %shard_map.225 = (f32[128,1024]{1,0:T(8,128)S(1)}, bf16[1024,128]{1,0:T(8,128)(2,1)S(1)}, f32[2,1024]{1,0:T(2,128)S(1)}) custom-call(s32[2]{0:T(128)S(1)} %compare_select_fusion.2.sel_ref, s32[8,16]{1,0:T(8,128)S(1)} %reshape.107.key_ref, s32[16]{0:T(128)S(1)} %reshape_squeeze.3.query_ref, bf16[128,1024]{1,0:T(8,128)(2,1)S(1)} %get-tuple-element.169.q_ref, ...), custom_call_target="tpu_custom_call" | custom-call | flops 14000000000 | bytes 14000000 | tf_op jit(solution)/shard_map/pallas_call | solution.py:55
  79.1 4.5 %collective-permute-done.20.refs_17_ = bf16[240,960]{1,0:T(8,128)(2,1)S(1)} collective-permute-done((bf16[240,960]{1,0:T(8,128)(2,1)S(1)}, bf16[240,960]{1,0:T(8,128)(2,1)S(1)}, u32[]{:S(2)}, u32[]{:S(2)}) %collective-permute-start.20) | collective-permute-done | bytes 460832 | tf_op jit(solution)/shard_map/ppermute | solution.py:29
  83.7 2.1 collective-permute-done.19.refs_18_
  85.9 1.1 collective-permute-start.27
  87.0 1.3 collective-permute-start.26
  88.3 1.1 collective-permute-start.25
  89.4 6.7 %collective-permute-done.27.refs_6_ = bf16[1024,128]{1,0:T(8,128)(2,1)S(1)} collective-permute-done((bf16[1024,128]{1,0:T(8,128)(2,1)S(1)}, bf16[1024,128]{1,0:T(8,128)(2,1)S(1)}, u32[]{:S(2)}, u32[]{:S(2)}) %collective-permute-start.27) | collective-permute-done | bytes 262176 | tf_op jit(solution)/shard_map/ppermute | solution.py:29
  96.1 3.6 %collective-permute-done.26.refs_4_ = bf16[1024,128]{1,0:T(8,128)(2,1)S(1)} collective-permute-done((bf16[1024,128]{1,0:T(8,128)(2,1)S(1)}, bf16[1024,128]{1,0:T(8,128)(2,1)S(1)}, u32[]{:S(2)}, u32[]{:S(2)}) %collective-permute-start.26) | collective-permute-done | bytes 262176 | tf_op jit(solution)/shard_map/ppermute | solution.py:29
  101.4 1.7 collective-permute-done.29.refs_3_
  103.9 16.3 %shard_map.226 = (f32[128,960]{1,0:T(8,128)S(1)}, bf16[512,960]{1,0:T(8,128)(2,1)S(1)}, bf16[512,1024]{1,0:T(8,128)(2,1)S(1)}, f32[8,960]{1,0:T(8,128)S(1)}, bf1...) custom-call(s32[3]{0:T(128)S(1)} %copy-done.2, ...), custom_call_target="tpu_custom_call" | custom-call | flops 16999999488 | bytes 17000000 | tf_op jit(solution)/shard_map/pallas_call | solution.py:55
  120.5 2.5 %collective-permute-done.34.cross_ref = bf16[512,1024]{1,0:T(8,128)(2,1)S(1)} collective-permute-done((bf16[512,1024]{1,0:T(8,128)(2,1)S(1)}, bf16[512,1024]{1,0:T(8,128)(2,1)S(1)}, u32[]{:S(2)}, u32[]{:S(2)}) %collective-permute-start.34) | collective-permute-done | bytes 1048608 | tf_op jit(solution)/shard_map/ppermute | solution.py:29
  123.2 1.1 collective-permute-start.36
  125.0 1.8 collective-permute-start.38
  127.1 3.1 %shard_map.228 = (bf16[1024,1024]{1,0:T(8,128)(2,1)S(1)}, bf16[1024,960]{1,0:T(8,128)(2,1)S(1)}, bf16[512,960]{1,0:T(8,128)(2,1)S(1)}, bf16[512,1024]{1,0:T(8,128)(2,1)S(1)}) custom-call(s32[3]{0:T(128)S(1)} %copy-done.2, bf16[1024,128]{1,0:T(8,128)(2,1)S(1)} %get-tuple-element.186.refs_0_, bf16[1024,128]{1,0:T(8,128)(2,1)S(1)} %collective-permute-done.28.refs_1_, ...), custom_call_target="tpu_custom_call" | custom-call | flops 5000000000 | bytes 5000000 | tf_op jit(solution)/shard_map/pallas_call | solution.py:55
  130.3 2.1 collective-permute-done.36.refs_1_
  133.2 4.8 %collective-permute-done.38.refs_3_ = bf16[128,960]{1,0:T(8,128)(2,1)S(1)} collective-permute-done((bf16[128,960]{1,0:T(8,128)(2,1)S(1)}, bf16[128,960]{1,0:T(8,128)(2,1)S(1)}, u32[]{:S(2)}, u32[]{:S(2)}) %collective-permute-start.38) | collective-permute-done | bytes 245792 | tf_op jit(solution)/shard_map/ppermute | solution.py:29
  138.0 1.2 collective-permute-done.35.in_ref
  139.2 1.5 shard_map.229
  141.3 1.2 collective-permute-done.39.cross_ref.refs_9_
  142.5 1.1 collective-permute-start.41
  144.3 1.8 collective-permute-start.43
  146.1 3.0 %collective-permute-start.45 = (bf16[240,960]{1,0:T(8,128)(2,1)S(1)}, bf16[240,960]{1,0:T(8,128)(2,1)S(1)}, u32[]{:S(2)}, u32[]{:S(2)}) collective-permute-start(bf16[240,960]{1,0:T(8,128)(2,1)S(1)} %shard_map.233), channel_id=1, source_target_pairs={{0,2},{1,3},{2,0},{3,1},{4,6},{5,7},{6,4},{7,5},{8,10},{9,11},{10,... | collective-permute-start | bytes 1382408 | tf_op jit(solution)/shard_map/ppermute | solution.py:29
  149.8 2.0 collective-permute-done.43.refs_12_
  152.6 17.5 %shard_map.232 = (f32[128,1024]{1,0:T(8,128)S(1)}, f32[4096,128]{1,0:T(8,128)S(1)}, bf16[4096,128]{1,0:T(8,128)(2,1)S(1)}, bf16[1024,128]{1,0:T(8,128)(2,1)S(1)}) custom-call(s32[2]{0:T(128)S(1)} %compare_select_fusion.2.sel_ref, s32[8,16]{1,0:T(8,128)S(1)} %reshape.107.key_ref, s32[16]{0:T(128)S(1)} %reshape_squeeze.3.query_ref, ...), custom_call_target="tpu_custom_call" | custom-call | flops 17999998976 | bytes 18000000 | tf_op jit(solution)/shard_map/pallas_call | solution.py:55
  170.5 1.7 collective-permute-done.44.refs_0_
  172.3 2.7 %collective-permute-done.47.cross_ref = bf16[4096,128]{1,0:T(8,128)(2,1)S(1)} collective-permute-done((bf16[4096,128]{1,0:T(8,128)(2,1)S(1)}, bf16[4096,128]{1,0:T(8,128)(2,1)S(1)}, u32[]{:S(2)}, u32[]{:S(2)}) %collective-permute-start.47) | collective-permute-done | bytes 1048608 | tf_op jit(solution)/shard_map/ppermute | solution.py:29
  176.0 1.4 collective-permute-start.49
  177.8 1.5 collective-permute-start.51
  181.3 16.1 %collective-permute-done.51.refs_2_ = bf16[1024,128]{1,0:T(8,128)(2,1)S(1)} collective-permute-done((bf16[1024,128]{1,0:T(8,128)(2,1)S(1)}, bf16[1024,128]{1,0:T(8,128)(2,1)S(1)}, u32[]{:S(2)}, u32[]{:S(2)}) %collective-permute-start.51) | collective-permute-done | bytes 262176 | tf_op jit(solution)/shard_map/ppermute | solution.py:29
  197.4 1.2 collective-permute-done.50.refs_1_
  198.6 3.5 %shard_map.237 = (bf16[512,960]{1,0:T(8,128)(2,1)S(1)}, bf16[512,1024]{1,0:T(8,128)(2,1)S(1)}, f32[256,384]{1,0:T(8,128)S(1)}, bf16[256,384]{1,0:T(8,128)(2,1)S(...) custom-call(s32[3]{0:T(128)S(1)} %copy-done.2, f32[128,1024]{1,0:T(8,128)S(1)} %get-tuple-element.259.dq_ref, ...), custom_call_target="tpu_custom_call" | custom-call | flops 8000000000 | bytes 8000000 | tf_op jit(solution)/shard_map/pallas_call | solution.py:55
  202.3 2.5 %collective-permute-done.54.cross_ref = bf16[512,1024]{1,0:T(8,128)(2,1)S(1)} collective-permute-done((bf16[512,1024]{1,0:T(8,128)(2,1)S(1)}, bf16[512,1024]{1,0:T(8,128)(2,1)S(1)}, u32[]{:S(2)}, u32[]{:S(2)}) %collective-permute-start.54) | collective-permute-done | bytes 1048608 | tf_op jit(solution)/shard_map/ppermute | solution.py:29
  205.1 1.7 collective-permute-start.55
  207.5 4.9 %collective-permute-start.56 = (bf16[256,384]{1,0:T(8,128)(2,1)S(1)}, bf16[256,384]{1,0:T(8,128)(2,1)S(1)}, u32[]{:S(2)}, u32[]{:S(2)}) collective-permute-start(bf16[256,384]{1,0:T(8,128)(2,1)S(1)} %get-tuple-element.271), channel_id=1, source_target_pairs={{0,1},{1,0},{2,3},{3,2},{4,5},{5,4},{6,7},{7,6},{8,9},{9,8},{10,11... | collective-permute-start | bytes 589832 | tf_op jit(solution)/shard_map/ppermute | solution.py:29
  212.4 2.4 collective-permute-start.58
  214.7 5.1 %collective-permute-done.56 = bf16[256,384]{1,0:T(8,128)(2,1)S(1)} collective-permute-done((bf16[256,384]{1,0:T(8,128)(2,1)S(1)}, bf16[256,384]{1,0:T(8,128)(2,1)S(1)}, u32[]{:S(2)}, u32[]{:S(2)}) %collective-permute-start.56) | collective-permute-done | bytes 196640 | tf_op jit(solution)/shard_map/ppermute | solution.py:29
  219.8 9.6 %collective-permute-done.57 = bf16[256,384]{1,0:T(8,128)(2,1)S(1)} collective-permute-done((bf16[256,384]{1,0:T(8,128)(2,1)S(1)}, bf16[256,384]{1,0:T(8,128)(2,1)S(1)}, u32[]{:S(2)}, u32[]{:S(2)}) %collective-permute-start.57) | collective-permute-done | bytes 196640 | tf_op jit(solution)/shard_map/ppermute | solution.py:29
  229.7 1.4 collective-permute-start.62
  231.1 1.3 collective-permute-start.61
  233.4 1.4 collective-permute-start.67
  234.8 5.7 %shard_map.241 = (f32[240,2560]{1,0:T(8,128)}, f32[240,2560]{1,0:T(8,128)}, f32[960,640]{1,0:T(8,128)}) custom-call(s32[3]{0:T(128)S(1)} %copy-done.2, bf16[240,1024]{1,0:T(8,128)(2,1)S(1)} %shard_map.236.m_ref, bf16[240,1024]{1,0:T(8,128)(2,1)S(1)} %collective-permute-done.48.x_ref, bf16[240,1024]{1,0:T(8,128)(2,1)S(1)} %collective-permute-done.49.y_ref, ...), custom_call_target="tpu_custom_call" | custom-call | flops 7000000000 | bytes 7000000 | tf_op jit(solution)/shard_map/pallas_call | solution.py:55
  240.4 1.9 collective-permute-done.61.refs_4_
  244.6 2.5 %shard_map.242 = (f32[240,960]{1,0:T(8,128)}, f32[320,240]{1,0:T(8,128)}, f32[320,240]{1,0:T(8,128)}, f32[240,960]{1,0:T(8,128)}, f32[1,240]{1,0:T(1,128)}, /*index=5*/f32[1,240]{1,0:T(1,128)}) custom-call(s32[3]{0:T(128)S(1)} %copy-done.2, bf16[256,384]{1,0:T(8,128)(2,1)S(1)} %add_convert_fusion.refs_0_, ...), custom_call_target="tpu_custom_call" | custom-call | flops 10000000 | bytes 10000 | tf_op jit(solution)/shard_map/pallas_call | solution.py:55
  247.8 1.2 shard_map.243
  (149 shorter events, 25.6 us)
Async XLA Ops:
  3.9 21.6 %collective-permute-start.9 = (bf16[256,384]{1,0:T(8,128)(2,1)}, bf16[256,384]{1,0:T(8,128)(2,1)}, u32[]{:S(2)}, u32[]{:S(2)}) collective-permute-start(bf16[256,384]{1,0:T(8,128)(2,1)} %shard_map.221.refs_8_), channel_id=1, source_target_pairs={{0,3},{1,2},{2,1},{3,0},{4,7},{5,6},{6,5},{7,4},{8,11},{9,10},{10,... | collective-permute-start | bytes 589832 | tf_op jit(solution)/shard_map/ppermute | solution.py:29
  9.0 17.1 %collective-permute-start.8 = (bf16[256,384]{1,0:T(8,128)(2,1)}, bf16[256,384]{1,0:T(8,128)(2,1)}, u32[]{:S(2)}, u32[]{:S(2)}) collective-permute-start(bf16[256,384]{1,0:T(8,128)(2,1)} %shard_map.221.refs_8_), channel_id=1, source_target_pairs={{0,2},{1,3},{2,0},{3,1},{4,6},{5,7},{6,4},{7,5},{8,10},{9,11},{10,... | collective-permute-start | bytes 589832 | tf_op jit(solution)/shard_map/ppermute | solution.py:29
  9.1 10.8 %collective-permute-start.2 = (bf16[128,960]{1,0:T(8,128)(2,1)S(1)}, bf16[128,960]{1,0:T(8,128)(2,1)S(1)}, u32[]{:S(2)}, u32[]{:S(2)}) collective-permute-start(bf16[128,960]{1,0:T(8,128)(2,1)S(1)} %copy.57.refs_2_), channel_id=1, source_target_pairs={{0,24},{1,25},{2,26},{3,27},{4,28},{5,29},{6,30},{7,31},{8,16},{9,... | collective-permute-start | bytes 737288 | tf_op jit(solution)/shard_map/ppermute | solution.py:29
  11.6 12.1 %collective-permute-start.1 = (bf16[128,960]{1,0:T(8,128)(2,1)S(1)}, bf16[128,960]{1,0:T(8,128)(2,1)}, u32[]{:S(2)}, u32[]{:S(2)}) collective-permute-start(bf16[128,960]{1,0:T(8,128)(2,1)S(1)} %copy.57.refs_2_), channel_id=1, source_target_pairs={{0,16},{1,17},{2,18},{3,19},{4,20},{5,21},{6,22},{7,23},{8,24},{9,... | collective-permute-start | bytes 737288 | tf_op jit(solution)/shard_map/ppermute | solution.py:29
  12.1 11.6 %collective-permute-start = (bf16[128,960]{1,0:T(8,128)(2,1)S(1)}, bf16[128,960]{1,0:T(8,128)(2,1)}, u32[]{:S(2)}, u32[]{:S(2)}) collective-permute-start(bf16[128,960]{1,0:T(8,128)(2,1)S(1)} %copy.57.refs_2_), channel_id=1, source_target_pairs={{0,8},{1,9},{2,10},{3,11},{4,12},{5,13},{6,14},{7,15},{8,0},{9,1},... | collective-permute-start | bytes 737288 | tf_op jit(solution)/shard_map/ppermute | solution.py:29
  20.0 9.6 %collective-permute-start.7 = (bf16[256,384]{1,0:T(8,128)(2,1)S(1)}, bf16[256,384]{1,0:T(8,128)(2,1)S(1)}, u32[]{:S(2)}, u32[]{:S(2)}) collective-permute-start(bf16[256,384]{1,0:T(8,128)(2,1)S(1)} %copy-done.8), channel_id=1, source_target_pairs={{0,1},{1,0},{2,3},{3,2},{4,5},{5,4},{6,7},{7,6},{8,9},{9,8},{10,11... | collective-permute-start | bytes 589832 | tf_op jit(solution)/shard_map/ppermute | solution.py:29
  24.8 4.7 %collective-permute-start.3 = (bf16[128,960]{1,0:T(8,128)(2,1)S(1)}, bf16[128,960]{1,0:T(8,128)(2,1)S(1)}, u32[]{:S(2)}, u32[]{:S(2)}) collective-permute-start(bf16[128,960]{1,0:T(8,128)(2,1)S(1)} %copy.61.refs_0_), channel_id=1, source_target_pairs={{0,4},{1,5},{2,6},{3,7},{4,0},{5,1},{6,2},{7,3},{8,12},{9,13},{10,... | collective-permute-start | bytes 737288 | tf_op jit(solution)/shard_map/ppermute | solution.py:29
  24.9 4.7 %collective-permute-start.4 = (bf16[128,960]{1,0:T(8,128)(2,1)}, bf16[128,960]{1,0:T(8,128)(2,1)S(1)}, u32[]{:S(2)}, u32[]{:S(2)}) collective-permute-start(bf16[128,960]{1,0:T(8,128)(2,1)} %collective-permute-done.refs_2_), channel_id=1, source_target_pairs={{0,4},{1,5},{2,6},{3,7},{4,0},{5,1},{6,2},{7,3},{8,12},{9,13},{10,... | collective-permute-start | bytes 737288 | tf_op jit(solution)/shard_map/ppermute | solution.py:29
  25.4 4.2 %collective-permute-start.5 = (bf16[128,960]{1,0:T(8,128)(2,1)}, bf16[128,960]{1,0:T(8,128)(2,1)S(1)}, u32[]{:S(2)}, u32[]{:S(2)}) collective-permute-start(bf16[128,960]{1,0:T(8,128)(2,1)} %collective-permute-done.1.refs_4_), channel_id=1, source_target_pairs={{0,4},{1,5},{2,6},{3,7},{4,0},{5,1},{6,2},{7,3},{8,12},{9,13},{10,... | collective-permute-start | bytes 737288 | tf_op jit(solution)/shard_map/ppermute | solution.py:29
  26.1 3.5 %collective-permute-start.6 = (bf16[128,960]{1,0:T(8,128)(2,1)S(1)}, bf16[128,960]{1,0:T(8,128)(2,1)S(1)}, u32[]{:S(2)}, u32[]{:S(2)}) collective-permute-start(bf16[128,960]{1,0:T(8,128)(2,1)S(1)} %collective-permute-done.2.refs_6_), channel_id=1, source_target_pairs={{0,4},{1,5},{2,6},{3,7},{4,0},{5,1},{6,2},{7,3},{8,12},{9,13},{10,... | collective-permute-start | bytes 737288 | tf_op jit(solution)/shard_map/ppermute | solution.py:29
  33.1 26.3 %collective-permute-start.11 = (bf16[256,1024]{1,0:T(8,128)(2,1)S(1)}, bf16[256,1024]{1,0:T(8,128)(2,1)S(1)}, u32[]{:S(2)}, u32[]{:S(2)}) collective-permute-start(bf16[256,1024]{1,0:T(8,128)(2,1)S(1)} %get-tuple-element.181.refs_8_), channel_id=1, source_target_pairs={{0,16},{1,17},{2,18},{3,19},{4,20},{5,21},{6,22},{7,23},{8,24},{9,... | collective-permute-start | bytes 1572872 | tf_op jit(solution)/shard_map/ppermute | solution.py:29
  34.6 24.8 %collective-permute-start.10 = (bf16[256,1024]{1,0:T(8,128)(2,1)S(1)}, bf16[256,1024]{1,0:T(8,128)(2,1)S(1)}, u32[]{:S(2)}, u32[]{:S(2)}) collective-permute-start(bf16[256,1024]{1,0:T(8,128)(2,1)S(1)} %get-tuple-element.181.refs_8_), channel_id=1, source_target_pairs={{0,8},{1,9},{2,10},{3,11},{4,12},{5,13},{6,14},{7,15},{8,0},{9,1},... | collective-permute-start | bytes 1572872 | tf_op jit(solution)/shard_map/ppermute | solution.py:29
  36.5 11.1 %collective-permute-start.14 = (bf16[1024,128]{1,0:T(8,128)(2,1)S(1)}, bf16[1024,128]{1,0:T(8,128)(2,1)S(1)}, u32[]{:S(2)}, u32[]{:S(2)}) collective-permute-start(bf16[1024,128]{1,0:T(8,128)(2,1)S(1)} %get-tuple-element.170.refs_0_), channel_id=1, source_target_pairs={{0,3},{1,2},{2,1},{3,0},{4,7},{5,6},{6,5},{7,4},{8,11},{9,10},{10,... | collective-permute-start | bytes 786440 | tf_op jit(solution)/shard_map/ppermute | solution.py:29
  38.9 20.5 %collective-permute-start.13 = (bf16[1024,128]{1,0:T(8,128)(2,1)S(1)}, bf16[1024,128]{1,0:T(8,128)(2,1)S(1)}, u32[]{:S(2)}, u32[]{:S(2)}) collective-permute-start(bf16[1024,128]{1,0:T(8,128)(2,1)S(1)} %get-tuple-element.170.refs_0_), channel_id=1, source_target_pairs={{0,2},{1,3},{2,0},{3,1},{4,6},{5,7},{6,4},{7,5},{8,10},{9,11},{10,... | collective-permute-start | bytes 786440 | tf_op jit(solution)/shard_map/ppermute | solution.py:29
  38.9 20.5 %collective-permute-start.12 = (bf16[1024,128]{1,0:T(8,128)(2,1)S(1)}, bf16[1024,128]{1,0:T(8,128)(2,1)S(1)}, u32[]{:S(2)}, u32[]{:S(2)}) collective-permute-start(bf16[1024,128]{1,0:T(8,128)(2,1)S(1)} %get-tuple-element.170.refs_0_), channel_id=1, source_target_pairs={{0,1},{1,0},{2,3},{3,2},{4,5},{5,4},{6,7},{7,6},{8,9},{9,8},{10,11... | collective-permute-start | bytes 786440 | tf_op jit(solution)/shard_map/ppermute | solution.py:29
  59.5 4.1 %collective-permute-start.16 = (bf16[1024,128]{1,0:T(8,128)(2,1)S(1)}, bf16[1024,128]{1,0:T(8,128)(2,1)S(1)}, u32[]{:S(2)}, u32[]{:S(2)}) collective-permute-start(bf16[1024,128]{1,0:T(8,128)(2,1)S(1)} %collective-permute-done.12.refs_1_), channel_id=1, source_target_pairs={{0,4},{1,5},{2,6},{3,7},{4,0},{5,1},{6,2},{7,3},{8,12},{9,13},{10,... | collective-permute-start | bytes 786440 | tf_op jit(solution)/shard_map/ppermute | solution.py:29
  60.0 5.1 %collective-permute-start.17 = (bf16[1024,128]{1,0:T(8,128)(2,1)S(1)}, bf16[1024,128]{1,0:T(8,128)(2,1)S(1)}, u32[]{:S(2)}, u32[]{:S(2)}) collective-permute-start(bf16[1024,128]{1,0:T(8,128)(2,1)S(1)} %collective-permute-done.13.refs_2_), channel_id=1, source_target_pairs={{0,4},{1,5},{2,6},{3,7},{4,0},{5,1},{6,2},{7,3},{8,12},{9,13},{10,... | collective-permute-start | bytes 786440 | tf_op jit(solution)/shard_map/ppermute | solution.py:29
  60.1 5.0 %collective-permute-start.18 = (bf16[1024,128]{1,0:T(8,128)(2,1)S(1)}, bf16[1024,128]{1,0:T(8,128)(2,1)S(1)}, u32[]{:S(2)}, u32[]{:S(2)}) collective-permute-start(bf16[1024,128]{1,0:T(8,128)(2,1)S(1)} %collective-permute-done.14.refs_3_), channel_id=1, source_target_pairs={{0,4},{1,5},{2,6},{3,7},{4,0},{5,1},{6,2},{7,3},{8,12},{9,13},{10,... | collective-permute-start | bytes 786440 | tf_op jit(solution)/shard_map/ppermute | solution.py:29
  60.5 23.1 %collective-permute-start.20 = (bf16[240,960]{1,0:T(8,128)(2,1)S(1)}, bf16[240,960]{1,0:T(8,128)(2,1)S(1)}, u32[]{:S(2)}, u32[]{:S(2)}) collective-permute-start(bf16[240,960]{1,0:T(8,128)(2,1)S(1)} %copy-done.7), channel_id=1, source_target_pairs={{0,1},{1,0},{2,3},{3,2},{4,5},{5,4},{6,7},{7,6},{8,9},{9,8},{10,11... | collective-permute-start | bytes 1382408 | tf_op jit(solution)/shard_map/ppermute | solution.py:29
  61.0 24.7 %collective-permute-start.19 = (bf16[240,960]{1,0:T(8,128)(2,1)S(1)}, bf16[240,960]{1,0:T(8,128)(2,1)S(1)}, u32[]{:S(2)}, u32[]{:S(2)}) collective-permute-start(bf16[240,960]{1,0:T(8,128)(2,1)S(1)} %copy-done.7), channel_id=1, source_target_pairs={{0,2},{1,3},{2,0},{3,1},{4,6},{5,7},{6,4},{7,5},{8,10},{9,11},{10,... | collective-permute-start | bytes 1382408 | tf_op jit(solution)/shard_map/ppermute | solution.py:29
  63.6 22.1 %collective-permute-start.21 = (bf16[256,1024]{1,0:T(8,128)(2,1)S(1)}, bf16[256,1024]{1,0:T(8,128)(2,1)S(1)}, u32[]{:S(2)}, u32[]{:S(2)}) collective-permute-start(bf16[256,1024]{1,0:T(8,128)(2,1)S(1)} %collective-permute-done.10.refs_10_), channel_id=1, source_target_pairs={{0,16},{1,17},{2,18},{3,19},{4,20},{5,21},{6,22},{7,23},{8,24},{9,... | collective-permute-start | bytes 1572872 | tf_op jit(solution)/shard_map/ppermute | solution.py:29
  65.1 20.7 %collective-permute-start.22 = (bf16[256,1024]{1,0:T(8,128)(2,1)S(1)}, bf16[256,1024]{1,0:T(8,128)(2,1)S(1)}, u32[]{:S(2)}, u32[]{:S(2)}) collective-permute-start(bf16[256,1024]{1,0:T(8,128)(2,1)S(1)} %get-tuple-element.181.refs_8_), channel_id=1, source_target_pairs={{0,4},{1,5},{2,6},{3,7},{4,0},{5,1},{6,2},{7,3},{8,12},{9,13},{10,... | collective-permute-start | bytes 1572872 | tf_op jit(solution)/shard_map/ppermute | solution.py:29
  65.1 20.7 %collective-permute-start.23 = (bf16[256,1024]{1,0:T(8,128)(2,1)S(1)}, bf16[256,1024]{1,0:T(8,128)(2,1)S(1)}, u32[]{:S(2)}, u32[]{:S(2)}) collective-permute-start(bf16[256,1024]{1,0:T(8,128)(2,1)S(1)} %collective-permute-done.10.refs_10_), channel_id=1, source_target_pairs={{0,4},{1,5},{2,6},{3,7},{4,0},{5,1},{6,2},{7,3},{8,12},{9,13},{10,... | collective-permute-start | bytes 1572872 | tf_op jit(solution)/shard_map/ppermute | solution.py:29
  85.8 14.0 %collective-permute-start.24 = (bf16[240,960]{1,0:T(8,128)(2,1)S(1)}, bf16[240,960]{1,0:T(8,128)(2,1)S(1)}, u32[]{:S(2)}, u32[]{:S(2)}) collective-permute-start(bf16[240,960]{1,0:T(8,128)(2,1)S(1)} %collective-permute-done.19.refs_18_), channel_id=1, source_target_pairs={{0,1},{1,0},{2,3},{3,2},{4,5},{5,4},{6,7},{7,6},{8,9},{9,8},{10,11... | collective-permute-start | bytes 1382408 | tf_op jit(solution)/shard_map/ppermute | solution.py:29
  85.9 10.2 %collective-permute-start.27 = (bf16[1024,128]{1,0:T(8,128)(2,1)S(1)}, bf16[1024,128]{1,0:T(8,128)(2,1)S(1)}, u32[]{:S(2)}, u32[]{:S(2)}) collective-permute-start(bf16[1024,128]{1,0:T(8,128)(2,1)S(1)} %get-tuple-element.186.refs_0_), channel_id=1, source_target_pairs={{0,24},{1,25},{2,26},{3,27},{4,28},{5,29},{6,30},{7,31},{8,16},{9,... | collective-permute-start | bytes 786440 | tf_op jit(solution)/shard_map/ppermute | solution.py:29
  87.0 12.7 %collective-permute-start.26 = (bf16[1024,128]{1,0:T(8,128)(2,1)S(1)}, bf16[1024,128]{1,0:T(8,128)(2,1)S(1)}, u32[]{:S(2)}, u32[]{:S(2)}) collective-permute-start(bf16[1024,128]{1,0:T(8,128)(2,1)S(1)} %get-tuple-element.186.refs_0_), channel_id=1, source_target_pairs={{0,16},{1,17},{2,18},{3,19},{4,20},{5,21},{6,22},{7,23},{8,24},{9,... | collective-permute-start | bytes 786440 | tf_op jit(solution)/shard_map/ppermute | solution.py:29
  88.3 11.5 %collective-permute-start.25 = (bf16[1024,128]{1,0:T(8,128)(2,1)S(1)}, bf16[1024,128]{1,0:T(8,128)(2,1)S(1)}, u32[]{:S(2)}, u32[]{:S(2)}) collective-permute-start(bf16[1024,128]{1,0:T(8,128)(2,1)S(1)} %get-tuple-element.186.refs_0_), channel_id=1, source_target_pairs={{0,8},{1,9},{2,10},{3,11},{4,12},{5,13},{6,14},{7,15},{8,0},{9,1},... | collective-permute-start | bytes 786440 | tf_op jit(solution)/shard_map/ppermute | solution.py:29
  99.8 4.2 %collective-permute-start.32 = (bf16[256,1024]{1,0:T(8,128)(2,1)S(1)}, bf16[256,1024]{1,0:T(8,128)(2,1)S(1)}, u32[]{:S(2)}, u32[]{:S(2)}) collective-permute-start(bf16[256,1024]{1,0:T(8,128)(2,1)S(1)} %collective-permute-done.11.refs_12_), channel_id=1, source_target_pairs={{0,4},{1,5},{2,6},{3,7},{4,0},{5,1},{6,2},{7,3},{8,12},{9,13},{10,... | collective-permute-start | bytes 1572872 | tf_op jit(solution)/shard_map/ppermute | solution.py:29
  100.3 3.7 %collective-permute-start.33 = (bf16[256,1024]{1,0:T(8,128)(2,1)S(1)}, bf16[256,1024]{1,0:T(8,128)(2,1)S(1)}, u32[]{:S(2)}, u32[]{:S(2)}) collective-permute-start(bf16[256,1024]{1,0:T(8,128)(2,1)S(1)} %collective-permute-done.21.refs_14_), channel_id=1, source_target_pairs={{0,4},{1,5},{2,6},{3,7},{4,0},{5,1},{6,2},{7,3},{8,12},{9,13},{10,... | collective-permute-start | bytes 1572872 | tf_op jit(solution)/shard_map/ppermute | solution.py:29
  100.3 2.9 %collective-permute-start.29 = (bf16[1024,128]{1,0:T(8,128)(2,1)S(1)}, bf16[1024,128]{1,0:T(8,128)(2,1)S(1)}, u32[]{:S(2)}, u32[]{:S(2)}) collective-permute-start(bf16[1024,128]{1,0:T(8,128)(2,1)S(1)} %collective-permute-done.25.refs_2_), channel_id=1, source_target_pairs={{0,4},{1,5},{2,6},{3,7},{4,0},{5,1},{6,2},{7,3},{8,12},{9,13},{10,... | collective-permute-start | bytes 786440 | tf_op jit(solution)/shard_map/ppermute | solution.py:29
  100.8 2.8 %collective-permute-start.30 = (bf16[1024,128]{1,0:T(8,128)(2,1)S(1)}, bf16[1024,128]{1,0:T(8,128)(2,1)S(1)}, u32[]{:S(2)}, u32[]{:S(2)}) collective-permute-start(bf16[1024,128]{1,0:T(8,128)(2,1)S(1)} %collective-permute-done.26.refs_4_), channel_id=1, source_target_pairs={{0,4},{1,5},{2,6},{3,7},{4,0},{5,1},{6,2},{7,3},{8,12},{9,13},{10,... | collective-permute-start | bytes 786440 | tf_op jit(solution)/shard_map/ppermute | solution.py:29
  101.3 2.6 %collective-permute-start.31 = (bf16[1024,128]{1,0:T(8,128)(2,1)S(1)}, bf16[1024,128]{1,0:T(8,128)(2,1)S(1)}, u32[]{:S(2)}, u32[]{:S(2)}) collective-permute-start(bf16[1024,128]{1,0:T(8,128)(2,1)S(1)} %collective-permute-done.27.refs_6_), channel_id=1, source_target_pairs={{0,4},{1,5},{2,6},{3,7},{4,0},{5,1},{6,2},{7,3},{8,12},{9,13},{10,... | collective-permute-start | bytes 786440 | tf_op jit(solution)/shard_map/ppermute | solution.py:29
  120.3 2.7 %collective-permute-start.34 = (bf16[512,1024]{1,0:T(8,128)(2,1)S(1)}, bf16[512,1024]{1,0:T(8,128)(2,1)S(1)}, u32[]{:S(2)}, u32[]{:S(2)}) collective-permute-start(bf16[512,1024]{1,0:T(8,128)(2,1)S(1)} %get-tuple-element.199), channel_id=1, source_target_pairs={{0,4},{1,5},{2,6},{3,7},{4,0},{5,1},{6,2},{7,3},{8,12},{9,13},{10,... | collective-permute-start | bytes 3145736 | tf_op jit(solution)/shard_map/ppermute | solution.py:29
  123.2 9.2 %collective-permute-start.36 = (bf16[128,960]{1,0:T(8,128)(2,1)S(1)}, bf16[128,960]{1,0:T(8,128)(2,1)S(1)}, u32[]{:S(2)}, u32[]{:S(2)}) collective-permute-start(bf16[128,960]{1,0:T(8,128)(2,1)S(1)} %get-tuple-element.210), channel_id=1, source_target_pairs={{0,8},{1,9},{2,10},{3,11},{4,12},{5,13},{6,14},{7,15},{8,0},{9,1},... | collective-permute-start | bytes 737288 | tf_op jit(solution)/shard_map/ppermute | solution.py:29
  124.3 8.9 %collective-permute-start.37 = (bf16[128,960]{1,0:T(8,128)(2,1)S(1)}, bf16[128,960]{1,0:T(8,128)(2,1)S(1)}, u32[]{:S(2)}, u32[]{:S(2)}) collective-permute-start(bf16[128,960]{1,0:T(8,128)(2,1)S(1)} %get-tuple-element.211), channel_id=1, source_target_pairs={{0,16},{1,17},{2,18},{3,19},{4,20},{5,21},{6,22},{7,23},{8,24},{9,... | collective-permute-start | bytes 737288 | tf_op jit(solution)/shard_map/ppermute | solution.py:29
  125.0 13.0 %collective-permute-start.38 = (bf16[128,960]{1,0:T(8,128)(2,1)S(1)}, bf16[128,960]{1,0:T(8,128)(2,1)S(1)}, u32[]{:S(2)}, u32[]{:S(2)}) collective-permute-start(bf16[128,960]{1,0:T(8,128)(2,1)S(1)} %get-tuple-element.212), channel_id=1, source_target_pairs={{0,24},{1,25},{2,26},{3,27},{4,28},{5,29},{6,30},{7,31},{8,16},{9,... | collective-permute-start | bytes 737288 | tf_op jit(solution)/shard_map/ppermute | solution.py:29
  126.8 12.4 %collective-permute-start.35 = (bf16[240,960]{1,0:T(8,128)(2,1)S(1)}, bf16[240,960]{1,0:T(8,128)(2,1)S(1)}, u32[]{:S(2)}, u32[]{:S(2)}) collective-permute-start(bf16[240,960]{1,0:T(8,128)(2,1)S(1)} %get-tuple-element.209), channel_id=1, source_target_pairs={{0,1},{1,0},{2,3},{3,2},{4,5},{5,4},{6,7},{7,6},{8,9},{9,8},{10,11... | collective-permute-start | bytes 1382408 | tf_op jit(solution)/shard_map/ppermute | solution.py:29
  139.2 3.2 %collective-permute-start.40 = (bf16[512,1024]{1,0:T(8,128)(2,1)S(1)}, bf16[512,1024]{1,0:T(8,128)(2,1)S(1)}, u32[]{:S(2)}, u32[]{:S(2)}) collective-permute-start(bf16[512,1024]{1,0:T(8,128)(2,1)S(1)} %get-tuple-element.222), channel_id=1, source_target_pairs={{0,4},{1,5},{2,6},{3,7},{4,0},{5,1},{6,2},{7,3},{8,12},{9,13},{10,... | collective-permute-start | bytes 3145736 | tf_op jit(solution)/shard_map/ppermute | solution.py:29
  142.5 7.3 %collective-permute-start.41 = (bf16[256,256]{1,0:T(8,128)(2,1)S(1)}, bf16[256,256]{1,0:T(8,128)(2,1)S(1)}, u32[]{:S(2)}, u32[]{:S(2)}) collective-permute-start(bf16[256,256]{1,0:T(8,128)(2,1)S(1)} %get-tuple-element.228), channel_id=1, source_target_pairs={{0,8},{1,9},{2,10},{3,11},{4,12},{5,13},{6,14},{7,15},{8,0},{9,1},... | collective-permute-start | bytes 393224 | tf_op jit(solution)/shard_map/ppermute | solution.py:29
  143.6 6.2 %collective-permute-start.42 = (bf16[256,256]{1,0:T(8,128)(2,1)S(1)}, bf16[256,256]{1,0:T(8,128)(2,1)S(1)}, u32[]{:S(2)}, u32[]{:S(2)}) collective-permute-start(bf16[256,256]{1,0:T(8,128)(2,1)S(1)} %get-tuple-element.229), channel_id=1, source_target_pairs={{0,16},{1,17},{2,18},{3,19},{4,20},{5,21},{6,22},{7,23},{8,24},{9,... | collective-permute-start | bytes 393224 | tf_op jit(solution)/shard_map/ppermute | solution.py:29
  144.3 7.6 %collective-permute-start.43 = (bf16[256,256]{1,0:T(8,128)(2,1)S(1)}, bf16[256,256]{1,0:T(8,128)(2,1)S(1)}, u32[]{:S(2)}, u32[]{:S(2)}) collective-permute-start(bf16[256,256]{1,0:T(8,128)(2,1)S(1)} %get-tuple-element.230), channel_id=1, source_target_pairs={{0,24},{1,25},{2,26},{3,27},{4,28},{5,29},{6,30},{7,31},{8,16},{9,... | collective-permute-start | bytes 393224 | tf_op jit(solution)/shard_map/ppermute | solution.py:29
  146.1 24.4 %collective-permute-start.45 = (bf16[240,960]{1,0:T(8,128)(2,1)S(1)}, bf16[240,960]{1,0:T(8,128)(2,1)S(1)}, u32[]{:S(2)}, u32[]{:S(2)}) collective-permute-start(bf16[240,960]{1,0:T(8,128)(2,1)S(1)} %shard_map.233), channel_id=1, source_target_pairs={{0,2},{1,3},{2,0},{3,1},{4,6},{5,7},{6,4},{7,5},{8,10},{9,11},{10,... | collective-permute-start | bytes 1382408 | tf_op jit(solution)/shard_map/ppermute | solution.py:29
  149.4 22.9 %collective-permute-start.44 = (bf16[240,960]{1,0:T(8,128)(2,1)S(1)}, bf16[240,960]{1,0:T(8,128)(2,1)S(1)}, u32[]{:S(2)}, u32[]{:S(2)}) collective-permute-start(bf16[240,960]{1,0:T(8,128)(2,1)S(1)} %get-tuple-element.239), channel_id=1, source_target_pairs={{0,1},{1,0},{2,3},{3,2},{4,5},{5,4},{6,7},{7,6},{8,9},{9,8},{10,11... | collective-permute-start | bytes 1382408 | tf_op jit(solution)/shard_map/ppermute | solution.py:29
  151.9 20.4 %collective-permute-start.46 = (bf16[256,960]{1,0:T(8,128)(2,1)S(1)}, bf16[256,960]{1,0:T(8,128)(2,1)S(1)}, u32[]{:S(2)}, u32[]{:S(2)}) collective-permute-start(bf16[256,960]{1,0:T(8,128)(2,1)S(1)} %get-tuple-element.243), channel_id=1, source_target_pairs={{0,16},{1,17},{2,18},{3,19},{4,20},{5,21},{6,22},{7,23},{8,24},{9,... | collective-permute-start | bytes 1474568 | tf_op jit(solution)/shard_map/ppermute | solution.py:29
  172.3 2.7 %collective-permute-start.47 = (bf16[4096,128]{1,0:T(8,128)(2,1)S(1)}, bf16[4096,128]{1,0:T(8,128)(2,1)S(1)}, u32[]{:S(2)}, u32[]{:S(2)}) collective-permute-start(bf16[4096,128]{1,0:T(8,128)(2,1)S(1)} %get-tuple-element.244), channel_id=1, source_target_pairs={{0,4},{1,5},{2,6},{3,7},{4,0},{5,1},{6,2},{7,3},{8,12},{9,13},{10,... | collective-permute-start | bytes 3145736 | tf_op jit(solution)/shard_map/ppermute | solution.py:29
  176.0 22.6 %collective-permute-start.49 = (bf16[240,1024]{1,0:T(8,128)(2,1)S(1)}, bf16[240,1024]{1,0:T(8,128)(2,1)S(1)}, u32[]{:S(2)}, u32[]{:S(2)}) collective-permute-start(bf16[240,1024]{1,0:T(8,128)(2,1)S(1)} %shard_map.236.m_ref), channel_id=1, source_target_pairs={{0,16},{1,17},{2,18},{3,19},{4,20},{5,21},{6,22},{7,23},{8,24},{9,... | collective-permute-start | bytes 1474568 | tf_op jit(solution)/shard_map/ppermute | solution.py:29
  177.4 21.3 %collective-permute-start.48 = (bf16[240,1024]{1,0:T(8,128)(2,1)S(1)}, bf16[240,1024]{1,0:T(8,128)(2,1)S(1)}, u32[]{:S(2)}, u32[]{:S(2)}) collective-permute-start(bf16[240,1024]{1,0:T(8,128)(2,1)S(1)} %shard_map.236.m_ref), channel_id=1, source_target_pairs={{0,8},{1,9},{2,10},{3,11},{4,12},{5,13},{6,14},{7,15},{8,0},{9,1},... | collective-permute-start | bytes 1474568 | tf_op jit(solution)/shard_map/ppermute | solution.py:29
  177.8 19.6 %collective-permute-start.51 = (bf16[1024,128]{1,0:T(8,128)(2,1)S(1)}, bf16[1024,128]{1,0:T(8,128)(2,1)S(1)}, u32[]{:S(2)}, u32[]{:S(2)}) collective-permute-start(bf16[1024,128]{1,0:T(8,128)(2,1)S(1)} %get-tuple-element.256), channel_id=1, source_target_pairs={{0,2},{1,3},{2,0},{3,1},{4,6},{5,7},{6,4},{7,5},{8,10},{9,11},{10,... | collective-permute-start | bytes 786440 | tf_op jit(solution)/shard_map/ppermute | solution.py:29
  179.3 18.1 %collective-permute-start.52 = (bf16[1024,128]{1,0:T(8,128)(2,1)S(1)}, bf16[1024,128]{1,0:T(8,128)(2,1)S(1)}, u32[]{:S(2)}, u32[]{:S(2)}) collective-permute-start(bf16[1024,128]{1,0:T(8,128)(2,1)S(1)} %get-tuple-element.257), channel_id=1, source_target_pairs={{0,3},{1,2},{2,1},{3,0},{4,7},{5,6},{6,5},{7,4},{8,11},{9,10},{10,... | collective-permute-start | bytes 786440 | tf_op jit(solution)/shard_map/ppermute | solution.py:29
  180.3 18.4 %collective-permute-start.50 = (bf16[1024,128]{1,0:T(8,128)(2,1)S(1)}, bf16[1024,128]{1,0:T(8,128)(2,1)S(1)}, u32[]{:S(2)}, u32[]{:S(2)}) collective-permute-start(bf16[1024,128]{1,0:T(8,128)(2,1)S(1)} %get-tuple-element.245), channel_id=1, source_target_pairs={{0,1},{1,0},{2,3},{3,2},{4,5},{5,4},{6,7},{7,6},{8,9},{9,8},{10,11... | collective-permute-start | bytes 786440 | tf_op jit(solution)/shard_map/ppermute | solution.py:29
  202.1 2.7 %collective-permute-start.54 = (bf16[512,1024]{1,0:T(8,128)(2,1)S(1)}, bf16[512,1024]{1,0:T(8,128)(2,1)S(1)}, u32[]{:S(2)}, u32[]{:S(2)}) collective-permute-start(bf16[512,1024]{1,0:T(8,128)(2,1)S(1)} %get-tuple-element.268), channel_id=1, source_target_pairs={{0,4},{1,5},{2,6},{3,7},{4,0},{5,1},{6,2},{7,3},{8,12},{9,13},{10,... | collective-permute-start | bytes 3145736 | tf_op jit(solution)/shard_map/ppermute | solution.py:29
  205.1 24.3 %collective-permute-start.55 = (bf16[384,1024]{1,0:T(8,128)(2,1)S(1)}, bf16[384,1024]{1,0:T(8,128)(2,1)S(1)}, u32[]{:S(2)}, u32[]{:S(2)}) collective-permute-start(bf16[384,1024]{1,0:T(8,128)(2,1)S(1)} %get-tuple-element.270), channel_id=1, source_target_pairs={{0,8},{1,9},{2,10},{3,11},{4,12},{5,13},{6,14},{7,15},{8,0},{9,1},... | collective-permute-start | bytes 2359304 | tf_op jit(solution)/shard_map/ppermute | solution.py:29
  206.8 22.6 %collective-permute-start.53 = (bf16[240,1024]{1,0:T(8,128)(2,1)S(1)}, bf16[240,1024]{1,0:T(8,128)(2,1)S(1)}, u32[]{:S(2)}, u32[]{:S(2)}) collective-permute-start(bf16[240,1024]{1,0:T(8,128)(2,1)S(1)} %collective-permute-done.48.x_ref), channel_id=1, source_target_pairs={{0,16},{1,17},{2,18},{3,19},{4,20},{5,21},{6,22},{7,23},{8,24},{9,... | collective-permute-start | bytes 1474568 | tf_op jit(solution)/shard_map/ppermute | solution.py:29
  207.5 12.3 %collective-permute-start.56 = (bf16[256,384]{1,0:T(8,128)(2,1)S(1)}, bf16[256,384]{1,0:T(8,128)(2,1)S(1)}, u32[]{:S(2)}, u32[]{:S(2)}) collective-permute-start(bf16[256,384]{1,0:T(8,128)(2,1)S(1)} %get-tuple-element.271), channel_id=1, source_target_pairs={{0,1},{1,0},{2,3},{3,2},{4,5},{5,4},{6,7},{7,6},{8,9},{9,8},{10,11... | collective-permute-start | bytes 589832 | tf_op jit(solution)/shard_map/ppermute | solution.py:29
  212.4 17.0 %collective-permute-start.57 = (bf16[256,384]{1,0:T(8,128)(2,1)S(1)}, bf16[256,384]{1,0:T(8,128)(2,1)S(1)}, u32[]{:S(2)}, u32[]{:S(2)}) collective-permute-start(bf16[256,384]{1,0:T(8,128)(2,1)S(1)} %get-tuple-element.272), channel_id=1, source_target_pairs={{0,2},{1,3},{2,0},{3,1},{4,6},{5,7},{6,4},{7,5},{8,10},{9,11},{10,... | collective-permute-start | bytes 589832 | tf_op jit(solution)/shard_map/ppermute | solution.py:29
  212.4 17.0 %collective-permute-start.58 = (bf16[256,384]{1,0:T(8,128)(2,1)S(1)}, bf16[256,384]{1,0:T(8,128)(2,1)S(1)}, u32[]{:S(2)}, u32[]{:S(2)}) collective-permute-start(bf16[256,384]{1,0:T(8,128)(2,1)S(1)} %get-tuple-element.273), channel_id=1, source_target_pairs={{0,3},{1,2},{2,1},{3,0},{4,7},{5,6},{6,5},{7,4},{8,11},{9,10},{10,... | collective-permute-start | bytes 589832 | tf_op jit(solution)/shard_map/ppermute | solution.py:29
  229.6 5.2 %collective-permute-start.59 = (bf16[960,1024]{1,0:T(8,128)(2,1)S(1)}, bf16[960,1024]{1,0:T(8,128)(2,1)S(1)}, u32[]{:S(2)}, u32[]{:S(2)}) collective-permute-start(bf16[960,1024]{1,0:T(8,128)(2,1)S(1)} %pad_maximum_fusion), channel_id=1, source_target_pairs={{0,4},{1,5},{2,6},{3,7},{4,0},{5,1},{6,2},{7,3},{8,12},{9,13},{10,... | collective-permute-start | bytes 5898248 | tf_op jit(solution)/shard_map/ppermute | solution.py:29
  229.7 10.7 %collective-permute-start.62 = (bf16[256,384]{1,0:T(8,128)(2,1)S(1)}, bf16[256,384]{1,0:T(8,128)(2,1)S(1)}, u32[]{:S(2)}, u32[]{:S(2)}) collective-permute-start(bf16[256,384]{1,0:T(8,128)(2,1)S(1)} %add_convert_fusion.refs_0_), channel_id=1, source_target_pairs={{0,24},{1,25},{2,26},{3,27},{4,28},{5,29},{6,30},{7,31},{8,16},{9,... | collective-permute-start | bytes 589832 | tf_op jit(solution)/shard_map/ppermute | solution.py:29
  231.1 11.2 %collective-permute-start.61 = (bf16[256,384]{1,0:T(8,128)(2,1)S(1)}, bf16[256,384]{1,0:T(8,128)(2,1)S(1)}, u32[]{:S(2)}, u32[]{:S(2)}) collective-permute-start(bf16[256,384]{1,0:T(8,128)(2,1)S(1)} %add_convert_fusion.refs_0_), channel_id=1, source_target_pairs={{0,16},{1,17},{2,18},{3,19},{4,20},{5,21},{6,22},{7,23},{8,24},{9,... | collective-permute-start | bytes 589832 | tf_op jit(solution)/shard_map/ppermute | solution.py:29
  232.4 9.9 %collective-permute-start.60 = (bf16[256,384]{1,0:T(8,128)(2,1)S(1)}, bf16[256,384]{1,0:T(8,128)(2,1)S(1)}, u32[]{:S(2)}, u32[]{:S(2)}) collective-permute-start(bf16[256,384]{1,0:T(8,128)(2,1)S(1)} %add_convert_fusion.refs_0_), channel_id=1, source_target_pairs={{0,8},{1,9},{2,10},{3,11},{4,12},{5,13},{6,14},{7,15},{8,0},{9,1},... | collective-permute-start | bytes 589832 | tf_op jit(solution)/shard_map/ppermute | solution.py:29
  233.4 14.4 %collective-permute-start.67 = (bf16[128,960]{1,0:T(8,128)(2,1)S(1)}, bf16[128,960]{1,0:T(8,128)(2,1)S(1)}, u32[]{:S(2)}, u32[]{:S(2)}) collective-permute-start(bf16[128,960]{1,0:T(8,128)(2,1)S(1)} %get-tuple-element.289), channel_id=1, source_target_pairs={{0,16},{1,17},{2,18},{3,19},{4,20},{5,21},{6,22},{7,23},{8,24},{9,... | collective-permute-start | bytes 737288 | tf_op jit(solution)/shard_map/ppermute | solution.py:29
  242.3 1.9 collective-permute-start.63
  242.3 1.9 collective-permute-start.64
  242.8 1.8 collective-permute-start.66
  (16 other events, 110.1 us)
where the time goes:
time: 250 us; the launch traced here: 249 us
  waiting for transfers between devices  99.2 us (40%)
  Pallas kernels  77.1 us (31%)
  starting transfers between devices  61.7 us (25%)
  local copies, waits for them, and re-layouts  6.39 us (3%)
  other arithmetic  2.87 us (1%)
    ppermute x68, waiting for transfers between devices, exchange(): return lax.ppermute(array, AXES, [(i, i ^ mask) for i in range(count)])  99.2 us
    pallas_call x23, Pallas kernels, call(): pl.pallas_call(kernel, out_shape=tuple(outs), in_specs=specs, out_specs=t...  77.1 us
    ppermute x68, starting transfers between devices, exchange(): return lax.ppermute(array, AXES, [(i, i ^ mask) for i in range(count)])  61.7 us
  transfers between devices with their start and end apart: 68, of which 33 were waited for; matrix products, arithmetic and copies ran while one was open for 3% of the time, Pallas kernels for 20%

commit v1 on v0

--- a/solution.py
+++ b/solution.py
@@ -977,15 +977,15 @@
         tp = at_ref[0]
         total = jnp.zeros((16, 3 * OWN), f32)
         for j in range(TP):
-            hold[tp ^ j] = parts[j][...].astype(f32)
+            hold[tp ^ j] = parts[j][...]
             total = total + parts[j][pl.ds(d_rows, 16), :].astype(f32)
         one_ref[...] = total[0:1, :d_rows]
         two_ref[...] = total[1:2, :d_rows]
         heads = [hold[c][:d_rows, :OWN] for c in range(TP)]
-        q_ref[...] = jnp.concatenate(heads, axis=1)[:, :width]
+        q_ref[...] = jnp.concatenate(heads, axis=1)[:, :width].astype(f32)
         heads = [hold[c][:d_rows, 2 * OWN :] for c in range(TP)]
-        o_ref[...] = jnp.concatenate(heads, axis=1)[:, :width]
-        kv = [hold[c][:d_rows, OWN : 2 * OWN] for c in range(TP)]
+        o_ref[...] = jnp.concatenate(heads, axis=1)[:, :width].astype(f32)
+        kv = [hold[c][:d_rows, OWN : 2 * OWN].astype(f32) for c in range(TP)]
         kv = [kv[0], kv[1] + kv[2], kv[3] + kv[4], kv[5], kv[6]]
         for c in range(KV_HEADS):
             turned = kv[c].T
@@ -1003,7 +1003,7 @@
             shape((1, d_rows), f32),
         ],
         [at, *slots],
-        scratch=[pltpu.VMEM((TP, d_rows + 16, 3 * OWN), f32)],
+        scratch=[pltpu.VMEM((TP, d_rows + 16, 3 * OWN), bf16)],
         limit=12,
         cost=0.01,
     )
@@ -1093,7 +1093,8 @@
         side_x, side_y, inputs, turned_query, *own_kv
     )
     other_kv = level(*[send(slot, nz) for slot in own_kv])
-    one, near = send(after(pack_two, *own_kv), 1), send(after(pack_two, *own_kv), 2)
+    near = send(after(pack_two, *own_kv), 2)
+    one = send(after(pack_two, *other_kv), 1)
     side_xy = send(side_x, mask_y)
     side_odd, odd_x = send(after(side, *other_kv), nz), send(after(side_x, *other_kv), nz)
     attended, attended_own, log_mass = attention_forward(

time: 250 us -> 249 us (level)
  no operation moved by 1% of the time
where the time goes in v1:
time: 249 us
  waiting for transfers between devices  97 us (39%)
  Pallas kernels  77 us (31%)
  starting transfers between devices  63.4 us (25%)
  local copies, waits for them, and re-layouts  6.39 us (3%)
  other arithmetic  2.87 us (1%)
    ppermute x68, waiting for transfers between devices, exchange(): return lax.ppermute(array, AXES, [(i, i ^ mask) for i in range(count)])  97 us
    pallas_call x23, Pallas kernels, call(): pl.pallas_call(kernel, out_shape=tuple(outs), in_specs=specs, out_specs=t...  77 us
    ppermute x68, starting transfers between devices, exchange(): return lax.ppermute(array, AXES, [(i, i ^ mask) for i in range(count)])  63.4 us
  transfers between devices with their start and end apart: 68, of which 33 were waited for; matrix products, arithmetic and copies ran while one was open for 3% of the time, Pallas kernels for 20%

profile of v1, /device:TPU:0, one launch (start us, length us, event | category | flops | bytes accessed | tf_op | source)
XLA Modules:
  0.0 248.5 jit_solution(4907152069237445445)
XLA Ops:
  1.3 2.5 shard_map.221.refs_8_
  3.9 5.1 %collective-permute-start.9 = (bf16[256,384]{1,0:T(8,128)(2,1)}, bf16[256,384]{1,0:T(8,128)(2,1)}, u32[]{:S(2)}, u32[]{:S(2)}) collective-permute-start(bf16[256,384]{1,0:T(8,128)(2,1)} %shard_map.221.refs_8_), channel_id=1, source_target_pairs={{0,3},{1,2},{2,1},{3,0},{4,7},{5,6},{6,5},{7,4},{8,11},{9,10},{10,... | collective-permute-start | bytes 589832 | tf_op jit(solution)/shard_map/ppermute | solution.py:29
  9.1 2.5 %collective-permute-start.2 = (bf16[128,960]{1,0:T(8,128)(2,1)S(1)}, bf16[128,960]{1,0:T(8,128)(2,1)S(1)}, u32[]{:S(2)}, u32[]{:S(2)}) collective-permute-start(bf16[128,960]{1,0:T(8,128)(2,1)S(1)} %copy.57.refs_2_), channel_id=1, source_target_pairs={{0,24},{1,25},{2,26},{3,27},{4,28},{5,29},{6,30},{7,31},{8,16},{9,... | collective-permute-start | bytes 737288 | tf_op jit(solution)/shard_map/ppermute | solution.py:29
  14.7 1.3 copy-done.5
  15.9 1.9 shard_map.222.refs_16_
  18.8 1.1 copy.62.refs_14_.refs_5_
  20.7 3.1 %collective-permute-done.1.refs_4_ = bf16[128,960]{1,0:T(8,128)(2,1)} collective-permute-done((bf16[128,960]{1,0:T(8,128)(2,1)S(1)}, bf16[128,960]{1,0:T(8,128)(2,1)}, u32[]{:S(2)}, u32[]{:S(2)}) %collective-permute-start.1) | collective-permute-done | bytes 245792 | tf_op jit(solution)/shard_map/ppermute | solution.py:29
  23.7 1.1 copy.61.refs_0_
  26.1 1.9 fusion.2
  28.0 1.6 collective-permute-done.7.refs_9_
  29.6 3.5 %shard_map.223 = (bf16[1024,960]{1,0:T(8,128)(2,1)S(1)}, bf16[1024,128]{1,0:T(8,128)(2,1)S(1)}, bf16[960,256]{1,0:T(8,128)(2,1)S(1)}, bf16[256,1024]{1,0:T(8,128)(2,1)S(1)}, f32[8,960]{1,0:T(8,128)S(1)}) custom-call(s32[3]{0:T(128)S(1)} %copy-done.2, bf16[128,960]{1,0:T(8,128)(2,1)S(1)} %copy.61.refs_0_, ...), custom_call_target="tpu_custom_call" | custom-call | flops 4000000000 | bytes 4000000 | tf_op jit(solution)/shard_map/pallas_call | solution.py:55
  33.1 1.5 collective-permute-start.11
  34.6 1.9 collective-permute-start.10
  36.5 2.4 collective-permute-start.14
  38.9 2.0 collective-permute-start.12
  40.9 2.1 shard_map.224
  43.0 4.6 %collective-permute-done.14.refs_3_ = bf16[1024,128]{1,0:T(8,128)(2,1)S(1)} collective-permute-done((bf16[1024,128]{1,0:T(8,128)(2,1)S(1)}, bf16[1024,128]{1,0:T(8,128)(2,1)S(1)}, u32[]{:S(2)}, u32[]{:S(2)}) %collective-permute-start.14) | collective-permute-done | bytes 262176 | tf_op jit(solution)/shard_map/ppermute | solution.py:29
  47.7 11.7 %collective-permute-done.13.refs_2_ = bf16[1024,128]{1,0:T(8,128)(2,1)S(1)} collective-permute-done((bf16[1024,128]{1,0:T(8,128)(2,1)S(1)}, bf16[1024,128]{1,0:T(8,128)(2,1)S(1)}, u32[]{:S(2)}, u32[]{:S(2)}) %collective-permute-start.13) | collective-permute-done | bytes 262176 | tf_op jit(solution)/shard_map/ppermute | solution.py:29
  61.0 1.3 collective-permute-start.21
  62.4 2.8 %collective-permute-start.20 = (bf16[240,960]{1,0:T(8,128)(2,1)S(1)}, bf16[240,960]{1,0:T(8,128)(2,1)S(1)}, u32[]{:S(2)}, u32[]{:S(2)}) collective-permute-start(bf16[240,960]{1,0:T(8,128)(2,1)S(1)} %copy-done.7), channel_id=1, source_target_pairs={{0,1},{1,0},{2,3},{3,2},{4,5},{5,4},{6,7},{7,6},{8,9},{9,8},{10,11... | collective-permute-start | bytes 1382408 | tf_op jit(solution)/shard_map/ppermute | solution.py:29
  65.6 13.5 %shard_map.225 = (f32[128,1024]{1,0:T(8,128)S(1)}, bf16[1024,128]{1,0:T(8,128)(2,1)S(1)}, f32[2,1024]{1,0:T(2,128)S(1)}) custom-call(s32[2]{0:T(128)S(1)} %compare_select_fusion.2.sel_ref, s32[8,16]{1,0:T(8,128)S(1)} %reshape.107.key_ref, s32[16]{0:T(128)S(1)} %reshape_squeeze.3.query_ref, bf16[128,1024]{1,0:T(8,128)(2,1)S(1)} %get-tuple-element.170.q_ref, ...), custom_call_target="tpu_custom_call" | custom-call | flops 14000000000 | bytes 14000000 | tf_op jit(solution)/shard_map/pallas_call | solution.py:55
  79.2 6.0 %collective-permute-done.19.refs_18_ = bf16[240,960]{1,0:T(8,128)(2,1)S(1)} collective-permute-done((bf16[240,960]{1,0:T(8,128)(2,1)S(1)}, bf16[240,960]{1,0:T(8,128)(2,1)S(1)}, u32[]{:S(2)}, u32[]{:S(2)}) %collective-permute-start.19) | collective-permute-done | bytes 460832 | tf_op jit(solution)/shard_map/ppermute | solution.py:29
  85.2 1.3 collective-permute-done.20.refs_17_
  86.5 1.1 collective-permute-start.27
  88.3 1.7 collective-permute-start.25
  90.0 6.7 %collective-permute-done.27.refs_6_ = bf16[1024,128]{1,0:T(8,128)(2,1)S(1)} collective-permute-done((bf16[1024,128]{1,0:T(8,128)(2,1)S(1)}, bf16[1024,128]{1,0:T(8,128)(2,1)S(1)}, u32[]{:S(2)}, u32[]{:S(2)}) %collective-permute-start.27) | collective-permute-done | bytes 262176 | tf_op jit(solution)/shard_map/ppermute | solution.py:29
  96.7 3.4 %collective-permute-done.26.refs_4_ = bf16[1024,128]{1,0:T(8,128)(2,1)S(1)} collective-permute-done((bf16[1024,128]{1,0:T(8,128)(2,1)S(1)}, bf16[1024,128]{1,0:T(8,128)(2,1)S(1)}, u32[]{:S(2)}, u32[]{:S(2)}) %collective-permute-start.26) | collective-permute-done | bytes 262176 | tf_op jit(solution)/shard_map/ppermute | solution.py:29
  101.7 1.7 collective-permute-done.29.refs_3_
  104.2 16.3 %shard_map.226 = (f32[128,960]{1,0:T(8,128)S(1)}, bf16[512,960]{1,0:T(8,128)(2,1)S(1)}, bf16[512,1024]{1,0:T(8,128)(2,1)S(1)}, f32[8,960]{1,0:T(8,128)S(1)}, bf1...) custom-call(s32[3]{0:T(128)S(1)} %copy-done.2, ...), custom_call_target="tpu_custom_call" | custom-call | flops 16999999488 | bytes 17000000 | tf_op jit(solution)/shard_map/pallas_call | solution.py:55
  120.8 2.5 %collective-permute-done.34.cross_ref = bf16[512,1024]{1,0:T(8,128)(2,1)S(1)} collective-permute-done((bf16[512,1024]{1,0:T(8,128)(2,1)S(1)}, bf16[512,1024]{1,0:T(8,128)(2,1)S(1)}, u32[]{:S(2)}, u32[]{:S(2)}) %collective-permute-start.34) | collective-permute-done | bytes 1048608 | tf_op jit(solution)/shard_map/ppermute | solution.py:29
  123.5 1.0 collective-permute-start.36
  125.4 1.7 collective-permute-start.38
  127.1 1.7 collective-permute-start.35
  128.8 3.1 %shard_map.228 = (bf16[1024,1024]{1,0:T(8,128)(2,1)S(1)}, bf16[1024,960]{1,0:T(8,128)(2,1)S(1)}, bf16[512,960]{1,0:T(8,128)(2,1)S(1)}, bf16[512,1024]{1,0:T(8,128)(2,1)S(1)}) custom-call(s32[3]{0:T(128)S(1)} %copy-done.2, bf16[1024,128]{1,0:T(8,128)(2,1)S(1)} %get-tuple-element.188.refs_0_, bf16[1024,128]{1,0:T(8,128)(2,1)S(1)} %collective-permute-done.28.refs_1_, ...), custom_call_target="tpu_custom_call" | custom-call | flops 5000000000 | bytes 5000000 | tf_op jit(solution)/shard_map/pallas_call | solution.py:55
  133.4 4.8 %collective-permute-done.38.refs_3_ = bf16[128,960]{1,0:T(8,128)(2,1)S(1)} collective-permute-done((bf16[128,960]{1,0:T(8,128)(2,1)S(1)}, bf16[128,960]{1,0:T(8,128)(2,1)S(1)}, u32[]{:S(2)}, u32[]{:S(2)}) %collective-permute-start.38) | collective-permute-done | bytes 245792 | tf_op jit(solution)/shard_map/ppermute | solution.py:29
  138.3 1.3 collective-permute-done.35.in_ref
  139.5 1.5 shard_map.229
  141.6 1.2 collective-permute-done.39.cross_ref.refs_9_
  142.8 1.0 collective-permute-start.41
  144.6 1.8 collective-permute-start.43
  146.5 2.8 %collective-permute-start.45 = (bf16[240,960]{1,0:T(8,128)(2,1)S(1)}, bf16[240,960]{1,0:T(8,128)(2,1)S(1)}, u32[]{:S(2)}, u32[]{:S(2)}) collective-permute-start(bf16[240,960]{1,0:T(8,128)(2,1)S(1)} %shard_map.233), channel_id=1, source_target_pairs={{0,2},{1,3},{2,0},{3,1},{4,6},{5,7},{6,4},{7,5},{8,10},{9,11},{10,... | collective-permute-start | bytes 1382408 | tf_op jit(solution)/shard_map/ppermute | solution.py:29
  149.9 2.2 collective-permute-done.43.refs_12_
  152.9 17.5 %shard_map.232 = (f32[128,1024]{1,0:T(8,128)S(1)}, f32[4096,128]{1,0:T(8,128)S(1)}, bf16[4096,128]{1,0:T(8,128)(2,1)S(1)}, bf16[1024,128]{1,0:T(8,128)(2,1)S(1)}) custom-call(s32[2]{0:T(128)S(1)} %compare_select_fusion.2.sel_ref, s32[8,16]{1,0:T(8,128)S(1)} %reshape.107.key_ref, s32[16]{0:T(128)S(1)} %reshape_squeeze.3.query_ref, ...), custom_call_target="tpu_custom_call" | custom-call | flops 17999998976 | bytes 18000000 | tf_op jit(solution)/shard_map/pallas_call | solution.py:55
  171.3 2.7 %collective-permute-done.47.cross_ref = bf16[4096,128]{1,0:T(8,128)(2,1)S(1)} collective-permute-done((bf16[4096,128]{1,0:T(8,128)(2,1)S(1)}, bf16[4096,128]{1,0:T(8,128)(2,1)S(1)}, u32[]{:S(2)}, u32[]{:S(2)}) %collective-permute-start.47) | collective-permute-done | bytes 1048608 | tf_op jit(solution)/shard_map/ppermute | solution.py:29
  175.0 1.4 collective-permute-start.49
  176.7 2.7 %collective-permute-start.51 = (bf16[1024,128]{1,0:T(8,128)(2,1)S(1)}, bf16[1024,128]{1,0:T(8,128)(2,1)S(1)}, u32[]{:S(2)}, u32[]{:S(2)}) collective-permute-start(bf16[1024,128]{1,0:T(8,128)(2,1)S(1)} %get-tuple-element.258), channel_id=1, source_target_pairs={{0,2},{1,3},{2,0},{3,1},{4,6},{5,7},{6,4},{7,5},{8,10},{9,11},{10,... | collective-permute-start | bytes 786440 | tf_op jit(solution)/shard_map/ppermute | solution.py:29
  179.4 1.3 collective-permute-start.52
  180.7 17.2 %collective-permute-done.51.refs_2_ = bf16[1024,128]{1,0:T(8,128)(2,1)S(1)} collective-permute-done((bf16[1024,128]{1,0:T(8,128)(2,1)S(1)}, bf16[1024,128]{1,0:T(8,128)(2,1)S(1)}, u32[]{:S(2)}, u32[]{:S(2)}) %collective-permute-start.51) | collective-permute-done | bytes 262176 | tf_op jit(solution)/shard_map/ppermute | solution.py:29
  198.0 3.5 %shard_map.237 = (bf16[512,960]{1,0:T(8,128)(2,1)S(1)}, bf16[512,1024]{1,0:T(8,128)(2,1)S(1)}, f32[256,384]{1,0:T(8,128)S(1)}, bf16[256,384]{1,0:T(8,128)(2,1)S(...) custom-call(s32[3]{0:T(128)S(1)} %copy-done.2, f32[128,1024]{1,0:T(8,128)S(1)} %get-tuple-element.261.dq_ref, ...), custom_call_target="tpu_custom_call" | custom-call | flops 8000000000 | bytes 8000000 | tf_op jit(solution)/shard_map/pallas_call | solution.py:55
  201.7 2.5 %collective-permute-done.54.cross_ref = bf16[512,1024]{1,0:T(8,128)(2,1)S(1)} collective-permute-done((bf16[512,1024]{1,0:T(8,128)(2,1)S(1)}, bf16[512,1024]{1,0:T(8,128)(2,1)S(1)}, u32[]{:S(2)}, u32[]{:S(2)}) %collective-permute-start.54) | collective-permute-done | bytes 1048608 | tf_op jit(solution)/shard_map/ppermute | solution.py:29
  204.5 1.8 collective-permute-start.55
  206.9 4.9 %collective-permute-start.56 = (bf16[256,384]{1,0:T(8,128)(2,1)S(1)}, bf16[256,384]{1,0:T(8,128)(2,1)S(1)}, u32[]{:S(2)}, u32[]{:S(2)}) collective-permute-start(bf16[256,384]{1,0:T(8,128)(2,1)S(1)} %get-tuple-element.273), channel_id=1, source_target_pairs={{0,1},{1,0},{2,3},{3,2},{4,5},{5,4},{6,7},{7,6},{8,9},{9,8},{10,11... | collective-permute-start | bytes 589832 | tf_op jit(solution)/shard_map/ppermute | solution.py:29
  212.2 2.0 collective-permute-start.58
  214.2 5.2 %collective-permute-done.56 = bf16[256,384]{1,0:T(8,128)(2,1)S(1)} collective-permute-done((bf16[256,384]{1,0:T(8,128)(2,1)S(1)}, bf16[256,384]{1,0:T(8,128)(2,1)S(1)}, u32[]{:S(2)}, u32[]{:S(2)}) %collective-permute-start.56) | collective-permute-done | bytes 196640 | tf_op jit(solution)/shard_map/ppermute | solution.py:29
  219.4 9.6 %collective-permute-done.57 = bf16[256,384]{1,0:T(8,128)(2,1)S(1)} collective-permute-done((bf16[256,384]{1,0:T(8,128)(2,1)S(1)}, bf16[256,384]{1,0:T(8,128)(2,1)S(1)}, u32[]{:S(2)}, u32[]{:S(2)}) %collective-permute-start.57) | collective-permute-done | bytes 196640 | tf_op jit(solution)/shard_map/ppermute | solution.py:29
  229.3 1.2 collective-permute-start.62
  230.5 1.5 collective-permute-start.61
  231.9 0.9 collective-permute-start.60
  233.0 1.4 collective-permute-start.67
  234.4 5.7 %shard_map.241 = (f32[240,2560]{1,0:T(8,128)}, f32[240,2560]{1,0:T(8,128)}, f32[960,640]{1,0:T(8,128)}) custom-call(s32[3]{0:T(128)S(1)} %copy-done.2, bf16[240,1024]{1,0:T(8,128)(2,1)S(1)} %shard_map.236.m_ref, bf16[240,1024]{1,0:T(8,128)(2,1)S(1)} %collective-permute-done.48.x_ref, bf16[240,1024]{1,0:T(8,128)(2,1)S(1)} %collective-permute-done.49.y_ref, ...), custom_call_target="tpu_custom_call" | custom-call | flops 7000000000 | bytes 7000000 | tf_op jit(solution)/shard_map/pallas_call | solution.py:55
  240.1 1.8 collective-permute-done.61.refs_4_
  242.9 0.8 shard_map.239
  244.2 2.4 shard_map.242
  247.3 1.2 shard_map.243
  (149 shorter events, 23.9 us)
Async XLA Ops:
  3.9 21.6 %collective-permute-start.9 = (bf16[256,384]{1,0:T(8,128)(2,1)}, bf16[256,384]{1,0:T(8,128)(2,1)}, u32[]{:S(2)}, u32[]{:S(2)}) collective-permute-start(bf16[256,384]{1,0:T(8,128)(2,1)} %shard_map.221.refs_8_), channel_id=1, source_target_pairs={{0,3},{1,2},{2,1},{3,0},{4,7},{5,6},{6,5},{7,4},{8,11},{9,10},{10,... | collective-permute-start | bytes 589832 | tf_op jit(solution)/shard_map/ppermute | solution.py:29
  9.0 17.1 %collective-permute-start.8 = (bf16[256,384]{1,0:T(8,128)(2,1)}, bf16[256,384]{1,0:T(8,128)(2,1)}, u32[]{:S(2)}, u32[]{:S(2)}) collective-permute-start(bf16[256,384]{1,0:T(8,128)(2,1)} %shard_map.221.refs_8_), channel_id=1, source_target_pairs={{0,2},{1,3},{2,0},{3,1},{4,6},{5,7},{6,4},{7,5},{8,10},{9,11},{10,... | collective-permute-start | bytes 589832 | tf_op jit(solution)/shard_map/ppermute | solution.py:29
  9.1 10.8 %collective-permute-start.2 = (bf16[128,960]{1,0:T(8,128)(2,1)S(1)}, bf16[128,960]{1,0:T(8,128)(2,1)S(1)}, u32[]{:S(2)}, u32[]{:S(2)}) collective-permute-start(bf16[128,960]{1,0:T(8,128)(2,1)S(1)} %copy.57.refs_2_), channel_id=1, source_target_pairs={{0,24},{1,25},{2,26},{3,27},{4,28},{5,29},{6,30},{7,31},{8,16},{9,... | collective-permute-start | bytes 737288 | tf_op jit(solution)/shard_map/ppermute | solution.py:29
  11.6 12.1 %collective-permute-start.1 = (bf16[128,960]{1,0:T(8,128)(2,1)S(1)}, bf16[128,960]{1,0:T(8,128)(2,1)}, u32[]{:S(2)}, u32[]{:S(2)}) collective-permute-start(bf16[128,960]{1,0:T(8,128)(2,1)S(1)} %copy.57.refs_2_), channel_id=1, source_target_pairs={{0,16},{1,17},{2,18},{3,19},{4,20},{5,21},{6,22},{7,23},{8,24},{9,... | collective-permute-start | bytes 737288 | tf_op jit(solution)/shard_map/ppermute | solution.py:29
  12.1 11.6 %collective-permute-start = (bf16[128,960]{1,0:T(8,128)(2,1)S(1)}, bf16[128,960]{1,0:T(8,128)(2,1)}, u32[]{:S(2)}, u32[]{:S(2)}) collective-permute-start(bf16[128,960]{1,0:T(8,128)(2,1)S(1)} %copy.57.refs_2_), channel_id=1, source_target_pairs={{0,8},{1,9},{2,10},{3,11},{4,12},{5,13},{6,14},{7,15},{8,0},{9,1},... | collective-permute-start | bytes 737288 | tf_op jit(solution)/shard_map/ppermute | solution.py:29
  20.0 9.6 %collective-permute-start.7 = (bf16[256,384]{1,0:T(8,128)(2,1)S(1)}, bf16[256,384]{1,0:T(8,128)(2,1)S(1)}, u32[]{:S(2)}, u32[]{:S(2)}) collective-permute-start(bf16[256,384]{1,0:T(8,128)(2,1)S(1)} %copy-done.8), channel_id=1, source_target_pairs={{0,1},{1,0},{2,3},{3,2},{4,5},{5,4},{6,7},{7,6},{8,9},{9,8},{10,11... | collective-permute-start | bytes 589832 | tf_op jit(solution)/shard_map/ppermute | solution.py:29
  24.8 4.7 %collective-permute-start.3 = (bf16[128,960]{1,0:T(8,128)(2,1)S(1)}, bf16[128,960]{1,0:T(8,128)(2,1)S(1)}, u32[]{:S(2)}, u32[]{:S(2)}) collective-permute-start(bf16[128,960]{1,0:T(8,128)(2,1)S(1)} %copy.61.refs_0_), channel_id=1, source_target_pairs={{0,4},{1,5},{2,6},{3,7},{4,0},{5,1},{6,2},{7,3},{8,12},{9,13},{10,... | collective-permute-start | bytes 737288 | tf_op jit(solution)/shard_map/ppermute | solution.py:29
  24.9 4.7 %collective-permute-start.4 = (bf16[128,960]{1,0:T(8,128)(2,1)}, bf16[128,960]{1,0:T(8,128)(2,1)S(1)}, u32[]{:S(2)}, u32[]{:S(2)}) collective-permute-start(bf16[128,960]{1,0:T(8,128)(2,1)} %collective-permute-done.refs_2_), channel_id=1, source_target_pairs={{0,4},{1,5},{2,6},{3,7},{4,0},{5,1},{6,2},{7,3},{8,12},{9,13},{10,... | collective-permute-start | bytes 737288 | tf_op jit(solution)/shard_map/ppermute | solution.py:29
  25.4 4.2 %collective-permute-start.5 = (bf16[128,960]{1,0:T(8,128)(2,1)}, bf16[128,960]{1,0:T(8,128)(2,1)S(1)}, u32[]{:S(2)}, u32[]{:S(2)}) collective-permute-start(bf16[128,960]{1,0:T(8,128)(2,1)} %collective-permute-done.1.refs_4_), channel_id=1, source_target_pairs={{0,4},{1,5},{2,6},{3,7},{4,0},{5,1},{6,2},{7,3},{8,12},{9,13},{10,... | collective-permute-start | bytes 737288 | tf_op jit(solution)/shard_map/ppermute | solution.py:29
  26.1 3.5 %collective-permute-start.6 = (bf16[128,960]{1,0:T(8,128)(2,1)S(1)}, bf16[128,960]{1,0:T(8,128)(2,1)S(1)}, u32[]{:S(2)}, u32[]{:S(2)}) collective-permute-start(bf16[128,960]{1,0:T(8,128)(2,1)S(1)} %collective-permute-done.2.refs_6_), channel_id=1, source_target_pairs={{0,4},{1,5},{2,6},{3,7},{4,0},{5,1},{6,2},{7,3},{8,12},{9,13},{10,... | collective-permute-start | bytes 737288 | tf_op jit(solution)/shard_map/ppermute | solution.py:29
  33.1 26.3 %collective-permute-start.11 = (bf16[256,1024]{1,0:T(8,128)(2,1)S(1)}, bf16[256,1024]{1,0:T(8,128)(2,1)S(1)}, u32[]{:S(2)}, u32[]{:S(2)}) collective-permute-start(bf16[256,1024]{1,0:T(8,128)(2,1)S(1)} %get-tuple-element.183.refs_8_), channel_id=1, source_target_pairs={{0,16},{1,17},{2,18},{3,19},{4,20},{5,21},{6,22},{7,23},{8,24},{9,... | collective-permute-start | bytes 1572872 | tf_op jit(solution)/shard_map/ppermute | solution.py:29
  34.6 24.8 %collective-permute-start.10 = (bf16[256,1024]{1,0:T(8,128)(2,1)S(1)}, bf16[256,1024]{1,0:T(8,128)(2,1)S(1)}, u32[]{:S(2)}, u32[]{:S(2)}) collective-permute-start(bf16[256,1024]{1,0:T(8,128)(2,1)S(1)} %get-tuple-element.183.refs_8_), channel_id=1, source_target_pairs={{0,8},{1,9},{2,10},{3,11},{4,12},{5,13},{6,14},{7,15},{8,0},{9,1},... | collective-permute-start | bytes 1572872 | tf_op jit(solution)/shard_map/ppermute | solution.py:29
  36.5 11.1 %collective-permute-start.14 = (bf16[1024,128]{1,0:T(8,128)(2,1)S(1)}, bf16[1024,128]{1,0:T(8,128)(2,1)S(1)}, u32[]{:S(2)}, u32[]{:S(2)}) collective-permute-start(bf16[1024,128]{1,0:T(8,128)(2,1)S(1)} %get-tuple-element.171.refs_0_), channel_id=1, source_target_pairs={{0,3},{1,2},{2,1},{3,0},{4,7},{5,6},{6,5},{7,4},{8,11},{9,10},{10,... | collective-permute-start | bytes 786440 | tf_op jit(solution)/shard_map/ppermute | solution.py:29
  38.9 20.5 %collective-permute-start.13 = (bf16[1024,128]{1,0:T(8,128)(2,1)S(1)}, bf16[1024,128]{1,0:T(8,128)(2,1)S(1)}, u32[]{:S(2)}, u32[]{:S(2)}) collective-permute-start(bf16[1024,128]{1,0:T(8,128)(2,1)S(1)} %get-tuple-element.171.refs_0_), channel_id=1, source_target_pairs={{0,2},{1,3},{2,0},{3,1},{4,6},{5,7},{6,4},{7,5},{8,10},{9,11},{10,... | collective-permute-start | bytes 786440 | tf_op jit(solution)/shard_map/ppermute | solution.py:29
  38.9 20.5 %collective-permute-start.12 = (bf16[1024,128]{1,0:T(8,128)(2,1)S(1)}, bf16[1024,128]{1,0:T(8,128)(2,1)S(1)}, u32[]{:S(2)}, u32[]{:S(2)}) collective-permute-start(bf16[1024,128]{1,0:T(8,128)(2,1)S(1)} %get-tuple-element.171.refs_0_), channel_id=1, source_target_pairs={{0,1},{1,0},{2,3},{3,2},{4,5},{5,4},{6,7},{7,6},{8,9},{9,8},{10,11... | collective-permute-start | bytes 786440 | tf_op jit(solution)/shard_map/ppermute | solution.py:29
  59.5 2.9 %collective-permute-start.16 = (bf16[1024,128]{1,0:T(8,128)(2,1)S(1)}, bf16[1024,128]{1,0:T(8,128)(2,1)S(1)}, u32[]{:S(2)}, u32[]{:S(2)}) collective-permute-start(bf16[1024,128]{1,0:T(8,128)(2,1)S(1)} %collective-permute-done.12.refs_1_), channel_id=1, source_target_pairs={{0,4},{1,5},{2,6},{3,7},{4,0},{5,1},{6,2},{7,3},{8,12},{9,13},{10,... | collective-permute-start | bytes 786440 | tf_op jit(solution)/shard_map/ppermute | solution.py:29
  60.0 2.4 collective-permute-start.17
  60.1 2.3 collective-permute-start.18
  60.5 24.7 %collective-permute-start.19 = (bf16[240,960]{1,0:T(8,128)(2,1)S(1)}, bf16[240,960]{1,0:T(8,128)(2,1)S(1)}, u32[]{:S(2)}, u32[]{:S(2)}) collective-permute-start(bf16[240,960]{1,0:T(8,128)(2,1)S(1)} %copy-done.7), channel_id=1, source_target_pairs={{0,2},{1,3},{2,0},{3,1},{4,6},{5,7},{6,4},{7,5},{8,10},{9,11},{10,... | collective-permute-start | bytes 1382408 | tf_op jit(solution)/shard_map/ppermute | solution.py:29
  61.0 24.2 %collective-permute-start.21 = (bf16[256,1024]{1,0:T(8,128)(2,1)S(1)}, bf16[256,1024]{1,0:T(8,128)(2,1)S(1)}, u32[]{:S(2)}, u32[]{:S(2)}) collective-permute-start(bf16[256,1024]{1,0:T(8,128)(2,1)S(1)} %collective-permute-done.10.refs_10_), channel_id=1, source_target_pairs={{0,16},{1,17},{2,18},{3,19},{4,20},{5,21},{6,22},{7,23},{8,24},{9,... | collective-permute-start | bytes 1572872 | tf_op jit(solution)/shard_map/ppermute | solution.py:29
  62.4 24.1 %collective-permute-start.20 = (bf16[240,960]{1,0:T(8,128)(2,1)S(1)}, bf16[240,960]{1,0:T(8,128)(2,1)S(1)}, u32[]{:S(2)}, u32[]{:S(2)}) collective-permute-start(bf16[240,960]{1,0:T(8,128)(2,1)S(1)} %copy-done.7), channel_id=1, source_target_pairs={{0,1},{1,0},{2,3},{3,2},{4,5},{5,4},{6,7},{7,6},{8,9},{9,8},{10,11... | collective-permute-start | bytes 1382408 | tf_op jit(solution)/shard_map/ppermute | solution.py:29
  65.1 21.3 %collective-permute-start.22 = (bf16[256,1024]{1,0:T(8,128)(2,1)S(1)}, bf16[256,1024]{1,0:T(8,128)(2,1)S(1)}, u32[]{:S(2)}, u32[]{:S(2)}) collective-permute-start(bf16[256,1024]{1,0:T(8,128)(2,1)S(1)} %get-tuple-element.183.refs_8_), channel_id=1, source_target_pairs={{0,4},{1,5},{2,6},{3,7},{4,0},{5,1},{6,2},{7,3},{8,12},{9,13},{10,... | collective-permute-start | bytes 1572872 | tf_op jit(solution)/shard_map/ppermute | solution.py:29
  65.1 21.3 %collective-permute-start.23 = (bf16[256,1024]{1,0:T(8,128)(2,1)S(1)}, bf16[256,1024]{1,0:T(8,128)(2,1)S(1)}, u32[]{:S(2)}, u32[]{:S(2)}) collective-permute-start(bf16[256,1024]{1,0:T(8,128)(2,1)S(1)} %collective-permute-done.10.refs_10_), channel_id=1, source_target_pairs={{0,4},{1,5},{2,6},{3,7},{4,0},{5,1},{6,2},{7,3},{8,12},{9,13},{10,... | collective-permute-start | bytes 1572872 | tf_op jit(solution)/shard_map/ppermute | solution.py:29
  86.5 13.6 %collective-permute-start.24 = (bf16[240,960]{1,0:T(8,128)(2,1)S(1)}, bf16[240,960]{1,0:T(8,128)(2,1)S(1)}, u32[]{:S(2)}, u32[]{:S(2)}) collective-permute-start(bf16[240,960]{1,0:T(8,128)(2,1)S(1)} %collective-permute-done.19.refs_18_), channel_id=1, source_target_pairs={{0,1},{1,0},{2,3},{3,2},{4,5},{5,4},{6,7},{7,6},{8,9},{9,8},{10,11... | collective-permute-start | bytes 1382408 | tf_op jit(solution)/shard_map/ppermute | solution.py:29
  86.5 10.2 %collective-permute-start.27 = (bf16[1024,128]{1,0:T(8,128)(2,1)S(1)}, bf16[1024,128]{1,0:T(8,128)(2,1)S(1)}, u32[]{:S(2)}, u32[]{:S(2)}) collective-permute-start(bf16[1024,128]{1,0:T(8,128)(2,1)S(1)} %get-tuple-element.188.refs_0_), channel_id=1, source_target_pairs={{0,24},{1,25},{2,26},{3,27},{4,28},{5,29},{6,30},{7,31},{8,16},{9,... | collective-permute-start | bytes 786440 | tf_op jit(solution)/shard_map/ppermute | solution.py:29
  87.6 12.5 %collective-permute-start.26 = (bf16[1024,128]{1,0:T(8,128)(2,1)S(1)}, bf16[1024,128]{1,0:T(8,128)(2,1)S(1)}, u32[]{:S(2)}, u32[]{:S(2)}) collective-permute-start(bf16[1024,128]{1,0:T(8,128)(2,1)S(1)} %get-tuple-element.188.refs_0_), channel_id=1, source_target_pairs={{0,16},{1,17},{2,18},{3,19},{4,20},{5,21},{6,22},{7,23},{8,24},{9,... | collective-permute-start | bytes 786440 | tf_op jit(solution)/shard_map/ppermute | solution.py:29
  88.3 11.8 %collective-permute-start.25 = (bf16[1024,128]{1,0:T(8,128)(2,1)S(1)}, bf16[1024,128]{1,0:T(8,128)(2,1)S(1)}, u32[]{:S(2)}, u32[]{:S(2)}) collective-permute-start(bf16[1024,128]{1,0:T(8,128)(2,1)S(1)} %get-tuple-element.188.refs_0_), channel_id=1, source_target_pairs={{0,8},{1,9},{2,10},{3,11},{4,12},{5,13},{6,14},{7,15},{8,0},{9,1},... | collective-permute-start | bytes 786440 | tf_op jit(solution)/shard_map/ppermute | solution.py:29
  100.1 4.2 %collective-permute-start.32 = (bf16[256,1024]{1,0:T(8,128)(2,1)S(1)}, bf16[256,1024]{1,0:T(8,128)(2,1)S(1)}, u32[]{:S(2)}, u32[]{:S(2)}) collective-permute-start(bf16[256,1024]{1,0:T(8,128)(2,1)S(1)} %collective-permute-done.11.refs_12_), channel_id=1, source_target_pairs={{0,4},{1,5},{2,6},{3,7},{4,0},{5,1},{6,2},{7,3},{8,12},{9,13},{10,... | collective-permute-start | bytes 1572872 | tf_op jit(solution)/shard_map/ppermute | solution.py:29
  100.6 3.7 %collective-permute-start.33 = (bf16[256,1024]{1,0:T(8,128)(2,1)S(1)}, bf16[256,1024]{1,0:T(8,128)(2,1)S(1)}, u32[]{:S(2)}, u32[]{:S(2)}) collective-permute-start(bf16[256,1024]{1,0:T(8,128)(2,1)S(1)} %collective-permute-done.21.refs_14_), channel_id=1, source_target_pairs={{0,4},{1,5},{2,6},{3,7},{4,0},{5,1},{6,2},{7,3},{8,12},{9,13},{10,... | collective-permute-start | bytes 1572872 | tf_op jit(solution)/shard_map/ppermute | solution.py:29
  100.7 2.8 %collective-permute-start.29 = (bf16[1024,128]{1,0:T(8,128)(2,1)S(1)}, bf16[1024,128]{1,0:T(8,128)(2,1)S(1)}, u32[]{:S(2)}, u32[]{:S(2)}) collective-permute-start(bf16[1024,128]{1,0:T(8,128)(2,1)S(1)} %collective-permute-done.25.refs_2_), channel_id=1, source_target_pairs={{0,4},{1,5},{2,6},{3,7},{4,0},{5,1},{6,2},{7,3},{8,12},{9,13},{10,... | collective-permute-start | bytes 786440 | tf_op jit(solution)/shard_map/ppermute | solution.py:29
  101.1 2.8 %collective-permute-start.30 = (bf16[1024,128]{1,0:T(8,128)(2,1)S(1)}, bf16[1024,128]{1,0:T(8,128)(2,1)S(1)}, u32[]{:S(2)}, u32[]{:S(2)}) collective-permute-start(bf16[1024,128]{1,0:T(8,128)(2,1)S(1)} %collective-permute-done.26.refs_4_), channel_id=1, source_target_pairs={{0,4},{1,5},{2,6},{3,7},{4,0},{5,1},{6,2},{7,3},{8,12},{9,13},{10,... | collective-permute-start | bytes 786440 | tf_op jit(solution)/shard_map/ppermute | solution.py:29
  101.6 2.6 %collective-permute-start.31 = (bf16[1024,128]{1,0:T(8,128)(2,1)S(1)}, bf16[1024,128]{1,0:T(8,128)(2,1)S(1)}, u32[]{:S(2)}, u32[]{:S(2)}) collective-permute-start(bf16[1024,128]{1,0:T(8,128)(2,1)S(1)} %collective-permute-done.27.refs_6_), channel_id=1, source_target_pairs={{0,4},{1,5},{2,6},{3,7},{4,0},{5,1},{6,2},{7,3},{8,12},{9,13},{10,... | collective-permute-start | bytes 786440 | tf_op jit(solution)/shard_map/ppermute | solution.py:29
  120.6 2.7 %collective-permute-start.34 = (bf16[512,1024]{1,0:T(8,128)(2,1)S(1)}, bf16[512,1024]{1,0:T(8,128)(2,1)S(1)}, u32[]{:S(2)}, u32[]{:S(2)}) collective-permute-start(bf16[512,1024]{1,0:T(8,128)(2,1)S(1)} %get-tuple-element.201), channel_id=1, source_target_pairs={{0,4},{1,5},{2,6},{3,7},{4,0},{5,1},{6,2},{7,3},{8,12},{9,13},{10,... | collective-permute-start | bytes 3145736 | tf_op jit(solution)/shard_map/ppermute | solution.py:29
  123.5 9.2 %collective-permute-start.36 = (bf16[128,960]{1,0:T(8,128)(2,1)S(1)}, bf16[128,960]{1,0:T(8,128)(2,1)S(1)}, u32[]{:S(2)}, u32[]{:S(2)}) collective-permute-start(bf16[128,960]{1,0:T(8,128)(2,1)S(1)} %get-tuple-element.212), channel_id=1, source_target_pairs={{0,8},{1,9},{2,10},{3,11},{4,12},{5,13},{6,14},{7,15},{8,0},{9,1},... | collective-permute-start | bytes 737288 | tf_op jit(solution)/shard_map/ppermute | solution.py:29
  124.6 8.9 %collective-permute-start.37 = (bf16[128,960]{1,0:T(8,128)(2,1)S(1)}, bf16[128,960]{1,0:T(8,128)(2,1)S(1)}, u32[]{:S(2)}, u32[]{:S(2)}) collective-permute-start(bf16[128,960]{1,0:T(8,128)(2,1)S(1)} %get-tuple-element.213), channel_id=1, source_target_pairs={{0,16},{1,17},{2,18},{3,19},{4,20},{5,21},{6,22},{7,23},{8,24},{9,... | collective-permute-start | bytes 737288 | tf_op jit(solution)/shard_map/ppermute | solution.py:29
  125.4 12.9 %collective-permute-start.38 = (bf16[128,960]{1,0:T(8,128)(2,1)S(1)}, bf16[128,960]{1,0:T(8,128)(2,1)S(1)}, u32[]{:S(2)}, u32[]{:S(2)}) collective-permute-start(bf16[128,960]{1,0:T(8,128)(2,1)S(1)} %get-tuple-element.214), channel_id=1, source_target_pairs={{0,24},{1,25},{2,26},{3,27},{4,28},{5,29},{6,30},{7,31},{8,16},{9,... | collective-permute-start | bytes 737288 | tf_op jit(solution)/shard_map/ppermute | solution.py:29
  127.1 12.4 %collective-permute-start.35 = (bf16[240,960]{1,0:T(8,128)(2,1)S(1)}, bf16[240,960]{1,0:T(8,128)(2,1)S(1)}, u32[]{:S(2)}, u32[]{:S(2)}) collective-permute-start(bf16[240,960]{1,0:T(8,128)(2,1)S(1)} %get-tuple-element.211), channel_id=1, source_target_pairs={{0,1},{1,0},{2,3},{3,2},{4,5},{5,4},{6,7},{7,6},{8,9},{9,8},{10,11... | collective-permute-start | bytes 1382408 | tf_op jit(solution)/shard_map/ppermute | solution.py:29
  139.5 3.2 %collective-permute-start.40 = (bf16[512,1024]{1,0:T(8,128)(2,1)S(1)}, bf16[512,1024]{1,0:T(8,128)(2,1)S(1)}, u32[]{:S(2)}, u32[]{:S(2)}) collective-permute-start(bf16[512,1024]{1,0:T(8,128)(2,1)S(1)} %get-tuple-element.224), channel_id=1, source_target_pairs={{0,4},{1,5},{2,6},{3,7},{4,0},{5,1},{6,2},{7,3},{8,12},{9,13},{10,... | collective-permute-start | bytes 3145736 | tf_op jit(solution)/shard_map/ppermute | solution.py:29
  142.8 7.1 %collective-permute-start.41 = (bf16[256,256]{1,0:T(8,128)(2,1)S(1)}, bf16[256,256]{1,0:T(8,128)(2,1)S(1)}, u32[]{:S(2)}, u32[]{:S(2)}) collective-permute-start(bf16[256,256]{1,0:T(8,128)(2,1)S(1)} %get-tuple-element.230), channel_id=1, source_target_pairs={{0,8},{1,9},{2,10},{3,11},{4,12},{5,13},{6,14},{7,15},{8,0},{9,1},... | collective-permute-start | bytes 393224 | tf_op jit(solution)/shard_map/ppermute | solution.py:29
  143.8 6.0 %collective-permute-start.42 = (bf16[256,256]{1,0:T(8,128)(2,1)S(1)}, bf16[256,256]{1,0:T(8,128)(2,1)S(1)}, u32[]{:S(2)}, u32[]{:S(2)}) collective-permute-start(bf16[256,256]{1,0:T(8,128)(2,1)S(1)} %get-tuple-element.231), channel_id=1, source_target_pairs={{0,16},{1,17},{2,18},{3,19},{4,20},{5,21},{6,22},{7,23},{8,24},{9,... | collective-permute-start | bytes 393224 | tf_op jit(solution)/shard_map/ppermute | solution.py:29
  144.6 7.5 %collective-permute-start.43 = (bf16[256,256]{1,0:T(8,128)(2,1)S(1)}, bf16[256,256]{1,0:T(8,128)(2,1)S(1)}, u32[]{:S(2)}, u32[]{:S(2)}) collective-permute-start(bf16[256,256]{1,0:T(8,128)(2,1)S(1)} %get-tuple-element.232), channel_id=1, source_target_pairs={{0,24},{1,25},{2,26},{3,27},{4,28},{5,29},{6,30},{7,31},{8,16},{9,... | collective-permute-start | bytes 393224 | tf_op jit(solution)/shard_map/ppermute | solution.py:29
  146.5 24.3 %collective-permute-start.45 = (bf16[240,960]{1,0:T(8,128)(2,1)S(1)}, bf16[240,960]{1,0:T(8,128)(2,1)S(1)}, u32[]{:S(2)}, u32[]{:S(2)}) collective-permute-start(bf16[240,960]{1,0:T(8,128)(2,1)S(1)} %shard_map.233), channel_id=1, source_target_pairs={{0,2},{1,3},{2,0},{3,1},{4,6},{5,7},{6,4},{7,5},{8,10},{9,11},{10,... | collective-permute-start | bytes 1382408 | tf_op jit(solution)/shard_map/ppermute | solution.py:29
  149.4 21.8 %collective-permute-start.44 = (bf16[240,960]{1,0:T(8,128)(2,1)S(1)}, bf16[240,960]{1,0:T(8,128)(2,1)S(1)}, u32[]{:S(2)}, u32[]{:S(2)}) collective-permute-start(bf16[240,960]{1,0:T(8,128)(2,1)S(1)} %get-tuple-element.241), channel_id=1, source_target_pairs={{0,1},{1,0},{2,3},{3,2},{4,5},{5,4},{6,7},{7,6},{8,9},{9,8},{10,11... | collective-permute-start | bytes 1382408 | tf_op jit(solution)/shard_map/ppermute | solution.py:29
  152.1 19.1 %collective-permute-start.46 = (bf16[256,960]{1,0:T(8,128)(2,1)S(1)}, bf16[256,960]{1,0:T(8,128)(2,1)S(1)}, u32[]{:S(2)}, u32[]{:S(2)}) collective-permute-start(bf16[256,960]{1,0:T(8,128)(2,1)S(1)} %get-tuple-element.245), channel_id=1, source_target_pairs={{0,16},{1,17},{2,18},{3,19},{4,20},{5,21},{6,22},{7,23},{8,24},{9,... | collective-permute-start | bytes 1474568 | tf_op jit(solution)/shard_map/ppermute | solution.py:29
  171.3 2.7 %collective-permute-start.47 = (bf16[4096,128]{1,0:T(8,128)(2,1)S(1)}, bf16[4096,128]{1,0:T(8,128)(2,1)S(1)}, u32[]{:S(2)}, u32[]{:S(2)}) collective-permute-start(bf16[4096,128]{1,0:T(8,128)(2,1)S(1)} %get-tuple-element.246), channel_id=1, source_target_pairs={{0,4},{1,5},{2,6},{3,7},{4,0},{5,1},{6,2},{7,3},{8,12},{9,13},{10,... | collective-permute-start | bytes 3145736 | tf_op jit(solution)/shard_map/ppermute | solution.py:29
  175.0 23.0 %collective-permute-start.49 = (bf16[240,1024]{1,0:T(8,128)(2,1)S(1)}, bf16[240,1024]{1,0:T(8,128)(2,1)S(1)}, u32[]{:S(2)}, u32[]{:S(2)}) collective-permute-start(bf16[240,1024]{1,0:T(8,128)(2,1)S(1)} %shard_map.236.m_ref), channel_id=1, source_target_pairs={{0,16},{1,17},{2,18},{3,19},{4,20},{5,21},{6,22},{7,23},{8,24},{9,... | collective-permute-start | bytes 1474568 | tf_op jit(solution)/shard_map/ppermute | solution.py:29
  176.4 21.6 %collective-permute-start.48 = (bf16[240,1024]{1,0:T(8,128)(2,1)S(1)}, bf16[240,1024]{1,0:T(8,128)(2,1)S(1)}, u32[]{:S(2)}, u32[]{:S(2)}) collective-permute-start(bf16[240,1024]{1,0:T(8,128)(2,1)S(1)} %shard_map.236.m_ref), channel_id=1, source_target_pairs={{0,8},{1,9},{2,10},{3,11},{4,12},{5,13},{6,14},{7,15},{8,0},{9,1},... | collective-permute-start | bytes 1474568 | tf_op jit(solution)/shard_map/ppermute | solution.py:29
  176.7 21.2 %collective-permute-start.51 = (bf16[1024,128]{1,0:T(8,128)(2,1)S(1)}, bf16[1024,128]{1,0:T(8,128)(2,1)S(1)}, u32[]{:S(2)}, u32[]{:S(2)}) collective-permute-start(bf16[1024,128]{1,0:T(8,128)(2,1)S(1)} %get-tuple-element.258), channel_id=1, source_target_pairs={{0,2},{1,3},{2,0},{3,1},{4,6},{5,7},{6,4},{7,5},{8,10},{9,11},{10,... | collective-permute-start | bytes 786440 | tf_op jit(solution)/shard_map/ppermute | solution.py:29
  179.4 18.5 %collective-permute-start.52 = (bf16[1024,128]{1,0:T(8,128)(2,1)S(1)}, bf16[1024,128]{1,0:T(8,128)(2,1)S(1)}, u32[]{:S(2)}, u32[]{:S(2)}) collective-permute-start(bf16[1024,128]{1,0:T(8,128)(2,1)S(1)} %get-tuple-element.259), channel_id=1, source_target_pairs={{0,3},{1,2},{2,1},{3,0},{4,7},{5,6},{6,5},{7,4},{8,11},{9,10},{10,... | collective-permute-start | bytes 786440 | tf_op jit(solution)/shard_map/ppermute | solution.py:29
  180.7 17.3 %collective-permute-start.50 = (bf16[1024,128]{1,0:T(8,128)(2,1)S(1)}, bf16[1024,128]{1,0:T(8,128)(2,1)S(1)}, u32[]{:S(2)}, u32[]{:S(2)}) collective-permute-start(bf16[1024,128]{1,0:T(8,128)(2,1)S(1)} %get-tuple-element.247), channel_id=1, source_target_pairs={{0,1},{1,0},{2,3},{3,2},{4,5},{5,4},{6,7},{7,6},{8,9},{9,8},{10,11... | collective-permute-start | bytes 786440 | tf_op jit(solution)/shard_map/ppermute | solution.py:29
  201.5 2.7 %collective-permute-start.54 = (bf16[512,1024]{1,0:T(8,128)(2,1)S(1)}, bf16[512,1024]{1,0:T(8,128)(2,1)S(1)}, u32[]{:S(2)}, u32[]{:S(2)}) collective-permute-start(bf16[512,1024]{1,0:T(8,128)(2,1)S(1)} %get-tuple-element.270), channel_id=1, source_target_pairs={{0,4},{1,5},{2,6},{3,7},{4,0},{5,1},{6,2},{7,3},{8,12},{9,13},{10,... | collective-permute-start | bytes 3145736 | tf_op jit(solution)/shard_map/ppermute | solution.py:29
  204.5 24.5 %collective-permute-start.55 = (bf16[384,1024]{1,0:T(8,128)(2,1)S(1)}, bf16[384,1024]{1,0:T(8,128)(2,1)S(1)}, u32[]{:S(2)}, u32[]{:S(2)}) collective-permute-start(bf16[384,1024]{1,0:T(8,128)(2,1)S(1)} %get-tuple-element.272), channel_id=1, source_target_pairs={{0,8},{1,9},{2,10},{3,11},{4,12},{5,13},{6,14},{7,15},{8,0},{9,1},... | collective-permute-start | bytes 2359304 | tf_op jit(solution)/shard_map/ppermute | solution.py:29
  206.3 22.7 %collective-permute-start.53 = (bf16[240,1024]{1,0:T(8,128)(2,1)S(1)}, bf16[240,1024]{1,0:T(8,128)(2,1)S(1)}, u32[]{:S(2)}, u32[]{:S(2)}) collective-permute-start(bf16[240,1024]{1,0:T(8,128)(2,1)S(1)} %collective-permute-done.48.x_ref), channel_id=1, source_target_pairs={{0,16},{1,17},{2,18},{3,19},{4,20},{5,21},{6,22},{7,23},{8,24},{9,... | collective-permute-start | bytes 1474568 | tf_op jit(solution)/shard_map/ppermute | solution.py:29
  206.9 12.4 %collective-permute-start.56 = (bf16[256,384]{1,0:T(8,128)(2,1)S(1)}, bf16[256,384]{1,0:T(8,128)(2,1)S(1)}, u32[]{:S(2)}, u32[]{:S(2)}) collective-permute-start(bf16[256,384]{1,0:T(8,128)(2,1)S(1)} %get-tuple-element.273), channel_id=1, source_target_pairs={{0,1},{1,0},{2,3},{3,2},{4,5},{5,4},{6,7},{7,6},{8,9},{9,8},{10,11... | collective-permute-start | bytes 589832 | tf_op jit(solution)/shard_map/ppermute | solution.py:29
  211.8 17.2 %collective-permute-start.57 = (bf16[256,384]{1,0:T(8,128)(2,1)S(1)}, bf16[256,384]{1,0:T(8,128)(2,1)S(1)}, u32[]{:S(2)}, u32[]{:S(2)}) collective-permute-start(bf16[256,384]{1,0:T(8,128)(2,1)S(1)} %get-tuple-element.274), channel_id=1, source_target_pairs={{0,2},{1,3},{2,0},{3,1},{4,6},{5,7},{6,4},{7,5},{8,10},{9,11},{10,... | collective-permute-start | bytes 589832 | tf_op jit(solution)/shard_map/ppermute | solution.py:29
  212.2 16.8 %collective-permute-start.58 = (bf16[256,384]{1,0:T(8,128)(2,1)S(1)}, bf16[256,384]{1,0:T(8,128)(2,1)S(1)}, u32[]{:S(2)}, u32[]{:S(2)}) collective-permute-start(bf16[256,384]{1,0:T(8,128)(2,1)S(1)} %get-tuple-element.275), channel_id=1, source_target_pairs={{0,3},{1,2},{2,1},{3,0},{4,7},{5,6},{6,5},{7,4},{8,11},{9,10},{10,... | collective-permute-start | bytes 589832 | tf_op jit(solution)/shard_map/ppermute | solution.py:29
  229.1 5.3 %collective-permute-start.59 = (bf16[960,1024]{1,0:T(8,128)(2,1)S(1)}, bf16[960,1024]{1,0:T(8,128)(2,1)S(1)}, u32[]{:S(2)}, u32[]{:S(2)}) collective-permute-start(bf16[960,1024]{1,0:T(8,128)(2,1)S(1)} %pad_maximum_fusion), channel_id=1, source_target_pairs={{0,4},{1,5},{2,6},{3,7},{4,0},{5,1},{6,2},{7,3},{8,12},{9,13},{10,... | collective-permute-start | bytes 5898248 | tf_op jit(solution)/shard_map/ppermute | solution.py:29
  229.3 10.7 %collective-permute-start.62 = (bf16[256,384]{1,0:T(8,128)(2,1)S(1)}, bf16[256,384]{1,0:T(8,128)(2,1)S(1)}, u32[]{:S(2)}, u32[]{:S(2)}) collective-permute-start(bf16[256,384]{1,0:T(8,128)(2,1)S(1)} %add_convert_fusion.refs_0_), channel_id=1, source_target_pairs={{0,24},{1,25},{2,26},{3,27},{4,28},{5,29},{6,30},{7,31},{8,16},{9,... | collective-permute-start | bytes 589832 | tf_op jit(solution)/shard_map/ppermute | solution.py:29
  230.5 11.4 %collective-permute-start.61 = (bf16[256,384]{1,0:T(8,128)(2,1)S(1)}, bf16[256,384]{1,0:T(8,128)(2,1)S(1)}, u32[]{:S(2)}, u32[]{:S(2)}) collective-permute-start(bf16[256,384]{1,0:T(8,128)(2,1)S(1)} %add_convert_fusion.refs_0_), channel_id=1, source_target_pairs={{0,16},{1,17},{2,18},{3,19},{4,20},{5,21},{6,22},{7,23},{8,24},{9,... | collective-permute-start | bytes 589832 | tf_op jit(solution)/shard_map/ppermute | solution.py:29
  231.9 10.0 %collective-permute-start.60 = (bf16[256,384]{1,0:T(8,128)(2,1)S(1)}, bf16[256,384]{1,0:T(8,128)(2,1)S(1)}, u32[]{:S(2)}, u32[]{:S(2)}) collective-permute-start(bf16[256,384]{1,0:T(8,128)(2,1)S(1)} %add_convert_fusion.refs_0_), channel_id=1, source_target_pairs={{0,8},{1,9},{2,10},{3,11},{4,12},{5,13},{6,14},{7,15},{8,0},{9,1},... | collective-permute-start | bytes 589832 | tf_op jit(solution)/shard_map/ppermute | solution.py:29
  233.0 14.4 %collective-permute-start.67 = (bf16[128,960]{1,0:T(8,128)(2,1)S(1)}, bf16[128,960]{1,0:T(8,128)(2,1)S(1)}, u32[]{:S(2)}, u32[]{:S(2)}) collective-permute-start(bf16[128,960]{1,0:T(8,128)(2,1)S(1)} %get-tuple-element.291), channel_id=1, source_target_pairs={{0,16},{1,17},{2,18},{3,19},{4,20},{5,21},{6,22},{7,23},{8,24},{9,... | collective-permute-start | bytes 737288 | tf_op jit(solution)/shard_map/ppermute | solution.py:29
  241.9 1.9 collective-permute-start.63
  241.9 1.9 collective-permute-start.64
  242.4 1.8 collective-permute-start.66
  (16 other events, 110.0 us)
